TPU v7x, 128 devices: a whole 4x4x4 slice. The times are simulated.
128 devices in a mesh: dp: 4 (over y_lo, core), ctx: 32 (over y_hi, x, z).
Axes of the slice: x: 4, y: 4 (y_hi: 2, y_lo: 2; y = y_hi * 2 + y_lo), z: 4, core: 2. Of those that a mesh axis runs over, the one named last changes fastest.
Arguments:
- tokens: bfloat16 [4, 4096, 960], P('dp', 'ctx'), may hold values from -6 to 6
- positions: int32 [4, 4096], P('dp', 'ctx'), may hold values from 0 to 4095, as said below
- w_query: bfloat16 [960, 960], P('dp'), may hold values from -0.1875 to 0.1875
- key_weight: bfloat16 [960, 320], P('dp'), may hold values from -0.1875 to 0.1875
- value_weight: bfloat16 [960, 320], P('dp'), may hold values from -0.1875 to 0.1875
- w_output: bfloat16 [960, 960], P('dp'), may hold values from -2 to 2
- gain_attn: bfloat16 [960], P('dp'), may hold values from 0.5 to 1.5
- w_gate: bfloat16 [960, 2560], P('dp'), may hold values from -0.1875 to 0.1875
- w_up: bfloat16 [960, 2560], P('dp'), may hold values from -0.1875 to 0.1875
- w_down: bfloat16 [2560, 960], P('dp'), may hold values from -0.125 to 0.125
- gain_mlp: bfloat16 [960], P('dp'), may hold values from 0.5 to 1.5
- cotangent: bfloat16 [4, 4096, 960], P('dp', 'ctx'), may hold values from -6 to 6
Outputs:
- output: bfloat16 [4, 4096, 960], P('dp', 'ctx')
- grad_input: bfloat16 [4, 4096, 960], P('dp', 'ctx')
- grad_query: float32 [960, 960], P('dp')
- grad_key: float32 [960, 320], P('dp')
- grad_value: float32 [960, 320], P('dp')
- grad_output: float32 [960, 960], P('dp')
- grad_gain_attn: float32 [960], P('dp')
- grad_gate: float32 [960, 2560], P('dp')
- grad_up: float32 [960, 2560], P('dp')
- grad_down: float32 [2560, 960], P('dp')
- grad_gain_mlp: float32 [960], P('dp')
Inputs may be any that keep to these rules, and one draw needn't show every extreme that they name: Each row holds every position 0 to 4095 exactly once; the 128 stored tokens of each device form two runs of 64 consecutive positions, ascending within a run.
All inputs are finite; a program needn't handle non-finite values.
Results may differ from a plain program's by a relative error of at most 0.035.
Values may be sent and summed in bfloat16 or wider, within the bound.
A program may use at most 192 MiB of HBM per device.

v0:
```python
import functools
import itertools
import math

import jax
import jax.numpy as jnp
from jax import lax
from jax.experimental import pallas as pl
from jax.experimental.pallas import tpu as pltpu
from jax.sharding import PartitionSpec as P

HQ = 15
KEY_VALUE_HEADS = 5
HEAD_SIZE = 64
QUERY_PER_KV = 3
MESH = pl.DeviceIdType.MESH
VMEM_LIMIT = 60 * 2**20
F32 = jnp.float32
BF16 = jnp.bfloat16
ROWS3 = 384


def coords():
    dp = lax.axis_index("dp")
    ctx = lax.axis_index("ctx")
    return dict(yl=dp // 2, c=dp % 2, yh=ctx // 16, x=(ctx // 4) % 4, z=ctx % 4)


def flip(t):
    return t + 1 - 2 * (t % 2)


def partner(co, d):
    new = dict(co)
    if d == "core":
        new["c"] = 1 - co["c"]
    elif d == "x1":
        new["x"] = flip(co["x"])
    elif d == "x3":
        new["x"] = 3 - co["x"]
    elif d == "z1":
        new["z"] = flip(co["z"])
    elif d == "z3":
        new["z"] = 3 - co["z"]
    else:
        if d in ("y1", "y3"):
            new["yl"] = 1 - co["yl"]
        if d in ("y2", "y3"):
            new["yh"] = 1 - co["yh"]
    return new


def device(co):
    return (co["yl"] * 2 + co["c"], co["yh"] * 16 + co["x"] * 4 + co["z"])


def spans(state, t):
    if state == "all":
        return [(0, 4)]
    if state == "both":
        return [(0, 2)]
    if state == "pair":
        return [(t - t % 2, 2)]
    if state == "anti":
        return [(t, 1), (3 - t, 1)]
    return [(t, 1)]


WIDTH = {"all": 4, "both": 2, "pair": 2, "anti": 2, "one": 1}


def less(state, d):
    new = dict(state)
    axis = d[0]
    if axis == "y":
        new["y"] = "one"
    elif state[axis] == "all":
        new[axis] = "anti" if d[1] == "1" else "pair"
    else:
        new[axis] = "one"
    return new


def more(state, d):
    new = dict(state)
    axis = d[0]
    if axis == "y":
        new["y"] = "both"
    elif state[axis] == "one":
        new[axis] = "pair" if d[1] == "1" else "anti"
    else:
        new[axis] = "all"
    return new


def boxes(state, co, ykey):
    out = []
    place_y = 0
    for ys, yn in spans(state["y"], co[ykey]):
        place_x = 0
        for xs, xn in spans(state["x"], co["x"]):
            place_z = 0
            for zs, zn in spans(state["z"], co["z"]):
                out.append(
                    (
                        (pl.ds(ys, yn), pl.ds(xs, xn), pl.ds(zs, zn)),
                        (pl.ds(place_y, yn), pl.ds(place_x, xn), pl.ds(place_z, zn)),
                        (yn, xn, zn),
                    )
                )
                place_z += zn
            place_x += xn
        place_y += yn
    return out


FULL = dict(y="both", x="all", z="all")
SINGLE = dict(y="one", x="one", z="one")


def order(ydim, part):
    dims = ["x1", "x3", "z1", "z3", ydim]
    return dims[part:] + dims[:part]


def rs_states(ydim, part):
    states = []
    state = FULL
    for d in order(ydim, part):
        state = less(state, d)
        states.append(state)
    return states


def rs_shapes(ydim, block):
    return [
        (WIDTH[s["y"]], WIDTH[s["x"]], WIDTH[s["z"]]) + block
        for part in range(5)
        for s in rs_states(ydim, part)
    ]


class Sems:
    def __init__(self, send, recv):
        self.send, self.recv, self.count = send, recv, 0

    def take(self):
        i = self.count
        self.count += 1
        return self.send.at[i], self.recv.at[i]

    def copy(self, src, dst, co):
        s, r = self.take()
        cp = pltpu.make_async_remote_copy(
            src_ref=src, dst_ref=dst, send_sem=s, recv_sem=r,
            device_id=device(co), device_id_type=MESH,
        )
        cp.start()
        return cp


def greet(co, dims):
    barrier = pltpu.get_barrier_semaphore()
    for d in dims:
        pl.semaphore_signal(
            barrier, inc=1, device_id=device(partner(co, d)), device_id_type=MESH
        )
    pl.semaphore_wait(barrier, len(dims))


class ReduceScatter:
    def __init__(self, acc, bufs, sems, co, ydim):
        self.acc, self.bufs, self.sems, self.co, self.ydim = acc, bufs, sems, co, ydim
        self.ykey = "yl" if ydim == "yl" else "yh"
        self.flying = {}
        self.sent = []

    def start(self, part, stage):
        d = order(self.ydim, part)[stage]
        state = rs_states(self.ydim, part)[stage]
        buf = self.bufs[part * 5 + stage]
        out = []
        if d == "yl":
            half = self.acc.shape[-2] // 2
            ways = [("y1", pl.ds(0, half)), ("y3", pl.ds(half, half))]
        else:
            ways = [(d, slice(None))]
        for way, rows in ways:
            to = partner(self.co, way)
            for box, place, _ in boxes(state, to, self.ykey):
                middle = (slice(None),) * (len(self.acc.shape) - 6)
                src = self.acc.at[box + (part,) + middle + (rows, slice(None))]
                dst = buf.at[place + middle + (rows, slice(None))]
                out.append(self.sems.copy(src, dst, to))
        self.flying[part, stage] = out
        self.sent += out

    def finish(self, part, stage):
        for cp in self.flying[part, stage]:
            cp.wait_recv()
        state = rs_states(self.ydim, part)[stage]
        buf = self.bufs[part * 5 + stage]
        for box, place, (yn, xn, zn) in boxes(state, self.co, self.ykey):
            (by, bx, bz), (py, px, pz) = box, place

            def add(i, carry):
                iy, ix, iz = i // (xn * zn), (i // zn) % xn, i % zn
                here = (by.start + iy, bx.start + ix, bz.start + iz, part)
                there = (py.start + iy, px.start + ix, pz.start + iz)
                self.acc[here] = (
                    self.acc[here].astype(F32) + buf[there].astype(F32)
                ).astype(BF16)
                return carry

            count = yn * xn * zn
            if count == 1:
                add(0, 0)
            else:
                lax.fori_loop(0, count, add, 0)

    def drain(self):
        for cp in self.sent:
            cp.wait_send()


class AllGather:
    def __init__(self, buf, sems, co, ydim="y2"):
        self.buf, self.sems, self.co, self.ydim = buf, sems, co, ydim
        self.flying = {}
        self.sent = []

    def start(self, part, stage):
        dims = order(self.ydim, part)
        state = SINGLE
        for d in dims[:stage]:
            state = more(state, d)
        to = partner(self.co, dims[stage])
        out = []
        for box, _, _ in boxes(state, self.co, "yh"):
            ref = self.buf.at[box + (part,)]
            out.append(self.sems.copy(ref, ref, to))
        self.flying[part, stage] = out
        self.sent += out

    def finish(self, part, stage):
        for cp in self.flying[part, stage]:
            cp.wait_recv()

    def drain(self):
        for cp in self.sent:
            cp.wait_send()


class PlaneGather:
    DIMS = ["x1", "x3", "z1", "z3"]

    def __init__(self, buf, sems, co):
        self.buf, self.sems, self.co = buf, sems, co
        self.flying = {}
        self.sent = []

    def first(self):
        co = self.co
        ref = self.buf.at[co["yh"], co["x"], co["z"]]
        self.sent.append(self.sems.copy(ref, ref, partner(co, "y2")))
        self.sent[0].wait_recv()

    def start(self, part, stage):
        dims = self.DIMS[part:] + self.DIMS[:part]
        state = dict(y="both", x="one", z="one")
        for d in dims[:stage]:
            state = more(state, d)
        to = partner(self.co, dims[stage])
        rows = pl.ds(32 * part, 32)
        groups = range(5) if stage == 3 else [slice(None)]
        for g in groups:
            out = []
            for box, _, _ in boxes(state, self.co, "yh"):
                ref = self.buf.at[box + (g, rows)]
                out.append(self.sems.copy(ref, ref, to))
            self.flying[part, stage, g if stage == 3 else 0] = out
            self.sent += out

    def finish(self, part, stage, g=0):
        for cp in self.flying[part, stage, g]:
            cp.wait_recv()

    def drain(self):
        for cp in self.sent:
            cp.wait_send()


class Gather:
    def __init__(self, items, sems, local, co):
        self.items, self.sems, self.local, self.co = items, sems, local, co
        self.waits = []

    def start(self):
        co = self.co
        me = co["yl"] * 2 + co["c"]
        self.stage = []
        for i, (src, dst, n, h) in enumerate(self.items):
            base = pl.multiple_of(me * n, 16)
            cp = pltpu.make_async_copy(src, dst.at[pl.ds(base, n)], self.local.at[i])
            cp.start()
            self.waits.append(cp)
        for src, dst, n, h in self.items:
            base = pl.multiple_of(me * n, 16)
            one = self.sems.copy(
                src.at[pl.ds(0, h)], dst.at[pl.ds(base, h)], partner(co, "y1")
            )
            two = None
            if h < n:
                two = self.sems.copy(
                    src.at[pl.ds(h, n - h)],
                    dst.at[pl.ds(pl.multiple_of(base + h, 16), n - h)],
                    partner(co, "y3"),
                )
            self.stage.append((one, two))
        for src, dst, n, h in self.items:
            base = pl.multiple_of(me * n, 16)
            self.waits.append(
                self.sems.copy(src, dst.at[pl.ds(base, n)], partner(co, "core"))
            )

    def forward(self, i):
        co = self.co
        src, dst, n, h = self.items[i]
        base = ((1 - co["yl"]) * 2 + co["c"]) * n
        for cp, at, size in zip(self.stage[i], (0, h), (h, n - h)):
            if cp is None:
                continue
            cp.wait_recv()
            ref = dst.at[pl.ds(pl.multiple_of(base + at, 16), size)]
            self.waits.append(self.sems.copy(ref, ref, partner(co, "core")))

    def finish(self):
        for one, two in self.stage:
            one.wait_send()
            if two is not None:
                two.wait_send()
        for cp in self.waits:
            cp.wait()


def params(cid):
    return pltpu.CompilerParams(
        collective_id=cid, has_side_effects=True, vmem_limit_bytes=VMEM_LIMIT
    )


def dma_sems(n):
    return pltpu.SemaphoreType.DMA((n,))


ANY = pl.BlockSpec(memory_space=pl.ANY)
INV = pl.BlockSpec(memory_space=pltpu.VMEM)


def first_kernel(w_ref, gain_ref, pos_ref, w_out, gain_out, pos_out, send, recv, local, ps, pr):
    co = coords()
    dp, me = lax.axis_index("dp"), lax.axis_index("ctx")
    barrier = pltpu.get_barrier_semaphore()
    for d in ("core", "y1"):
        pl.semaphore_signal(
            barrier, inc=1, device_id=device(partner(co, d)), device_id_type=MESH
        )

    def hello(i, carry):
        to = (me + 1 + i) % 32
        pl.semaphore_signal(barrier, inc=1, device_id=(dp, to), device_id_type=MESH)
        return carry

    lax.fori_loop(0, 31, hello, 0)
    pl.semaphore_signal(
        barrier, inc=1, device_id=device(partner(co, "y3")), device_id_type=MESH
    )
    pl.semaphore_wait(barrier, 34)
    gather = Gather(
        [(w_ref, w_out, 240, 128), (gain_ref, gain_out, 16, 16)],
        Sems(send, recv), local, co,
    )
    gather.start()

    def put(i, carry):
        to = (me + 1 + i) % 32
        pltpu.make_async_remote_copy(
            src_ref=pos_ref, dst_ref=pos_out.at[me], send_sem=ps, recv_sem=pr,
            device_id=(dp, to), device_id_type=MESH,
        ).start()
        return carry

    lax.fori_loop(0, 31, put, 0)
    own = pltpu.make_async_copy(pos_ref, pos_out.at[me], local.at[2])
    own.start()
    gather.forward(0)
    gather.forward(1)
    gather.finish()
    own.wait()
    block = pos_out.at[pl.ds(0, 31)]
    pltpu.make_async_copy(block, block, ps).wait()
    pltpu.make_async_copy(block, block, pr).wait()


def first_call(w_one, gains, pos):
    return pl.pallas_call(
        first_kernel,
        out_shape=(
            jax.ShapeDtypeStruct((960, 1600), BF16),
            jax.ShapeDtypeStruct((64, 256), BF16),
            jax.ShapeDtypeStruct((32, 8, 128), jnp.int32),
        ),
        in_specs=[INV] * 3,
        out_specs=[ANY] * 3,
        scratch_shapes=[
            dma_sems(8), dma_sems(8), dma_sems(3),
            pltpu.SemaphoreType.DMA, pltpu.SemaphoreType.DMA,
        ],
        compiler_params=params(1),
        name="gather_first",
    )(w_one, gains, pos)


CHUNK = 512


def over_dim0(left, right):
    return lax.dot_general(
        left, right, (((0,), (0,)), ((), ())), preferred_element_type=F32
    )


def forward_kernel(
    kv_ref, qt_ref, bias_ref, wo_ref, wg_ref, wu_ref, wd_ref,
    kv_all, u_ref, m_ref, l_ref, wo_all, wg_all, wu_all, wd_all,
    scores, send, recv, wsend, wrecv, local,
):
    co = coords()
    greet(co, ("x1", "x3", "z1", "z3", "y2", "core", "y1", "y3"))
    weights = Gather(
        [
            (wo_ref, wo_all, 240, 128),
            (wg_ref, wg_all, 240, 128),
            (wu_ref, wu_all, 240, 128),
            (wd_ref, wd_all, 640, 320),
        ],
        Sems(wsend, wrecv), local, co,
    )
    kv_all[co["yh"], co["x"], co["z"]] = kv_ref[...]
    ag = PlaneGather(kv_all, Sems(send, recv), co)
    ag.first()
    for part in range(4):
        ag.start(part, 0)
    weights.start()
    for stage in range(1, 4):
        for part in range(4):
            ag.finish(part, stage - 1)
            ag.start(part, stage)

    for g in range(KEY_VALUE_HEADS):
        for part in range(4):
            ag.finish(part, 3, g)
        if g > 0:
            weights.forward(g - 1)
        qt = qt_ref[g]

        def score(i, top):
            kv = kv_all[i // 4, i % 4, :, g].reshape(CHUNK, 128)
            s = jnp.dot(kv, qt, preferred_element_type=F32)
            b = bias_ref[pl.ds(i * CHUNK, CHUNK)]
            s = s + jnp.concatenate([b, b, b], axis=1)
            scores[pl.ds(i * CHUNK, CHUNK)] = s
            return jnp.maximum(top, jnp.max(s.reshape(CHUNK // 8, 8, ROWS3), axis=0))

        top = lax.fori_loop(0, 8, score, jnp.full((8, ROWS3), -1e30, F32))
        top = jnp.max(top, axis=0, keepdims=True)

        def weigh(i, carry):
            total, u = carry
            kv = kv_all[i // 4, i % 4, :, g].reshape(CHUNK, 128)
            e = jnp.exp(scores[pl.ds(i * CHUNK, CHUNK)] - top)
            total = total + jnp.sum(e.reshape(CHUNK // 8, 8, ROWS3), axis=0)
            return total, u + over_dim0(kv, e.astype(BF16))

        total, u = lax.fori_loop(
            0, 8, weigh, (jnp.zeros((8, ROWS3), F32), jnp.zeros((128, ROWS3), F32))
        )
        u_ref[g] = u
        m_ref[g] = top
        l_ref[g] = jnp.sum(total, axis=0, keepdims=True)
    ag.drain()
    weights.finish()


def forward_call(kv, qt, bias, wo, wg, wu, wd):
    shape = jax.ShapeDtypeStruct
    return pl.pallas_call(
        forward_kernel,
        out_shape=(
            shape((2, 4, 4, 5, 128, 128), BF16),
            shape((5, 128, ROWS3), F32),
            shape((5, 1, ROWS3), F32),
            shape((5, 1, ROWS3), F32),
            shape((960, 960), BF16),
            shape((960, 2560), BF16),
            shape((960, 2560), BF16),
            shape((2560, 960), BF16),
        ),
        in_specs=[INV] * 7,
        out_specs=[INV] * 4 + [ANY] * 4,
        scratch_shapes=[
            pltpu.VMEM((4096, ROWS3), F32),
            dma_sems(96), dma_sems(96), dma_sems(20), dma_sems(20), dma_sems(4),
        ],
        compiler_params=params(2),
        name="attention_forward",
    )(kv, qt, bias, wo, wg, wu, wd)


WIDE, TALL, GAIN = 240, 640, 256


def slab_shape(kind):
    return (640, 960) if kind == TALL else (kind, 2560)


def fold_block(own, got, yl, x, z, p, kind):
    if kind != TALL:
        rows = min(64, kind - 64 * x)
        lanes = pl.ds(pl.multiple_of(512 * p + 128 * z, 128), 128)
        at = (yl, pl.ds(64 * x, rows), lanes)
        s = own[at].astype(F32) + got[at].astype(F32)
        if rows < 64:
            s = jnp.concatenate([s, jnp.zeros((64 - rows, 128), F32)], axis=0)
        return s.astype(BF16)
    rows = pl.ds(pl.multiple_of(128 * p + 32 * x, 16), 32)
    halves = []
    for h in range(2):
        first = 256 * z + 128 * h
        count = min(128, 960 - first)
        at = (yl, rows, pl.ds(first, count))
        s = own[at].astype(F32) + got[at].astype(F32)
        if count < 128:
            s = jnp.concatenate([s, jnp.zeros((32, 128 - count), F32)], axis=1)
        halves.append(s)
    return jnp.concatenate(halves, axis=0).astype(BF16)


GRAD_DIMS = ("x1", "x3", "z1", "z3", "y1", "y2", "y3", "core")


def grad_scratch(kinds):
    n = len(kinds)
    blocks = [(2,) + slab_shape(kind) for kind in kinds]
    return (
        [pltpu.VMEM(b, BF16) for b in blocks]
        + [pltpu.VMEM(b, BF16) for b in blocks]
        + [pltpu.VMEM((2, 4, 4, 5, n, 64, 128), BF16)]
        + [pltpu.VMEM(s, BF16) for s in rs_shapes("yl", (n, 64, 128))]
        + [pltpu.VMEM((5, n, 32, 128), BF16)]
        + [dma_sems(64), dma_sems(64), dma_sems(2 * n), dma_sems(2 * n), dma_sems(2 * n)]
    )


def grad_scratch_count(kinds):
    return 2 * len(kinds) + 32


class GradSum:
    def __init__(self, kinds, slabs, scratch, co):
        n = len(kinds)
        self.kinds, self.slabs, self.co = kinds, slabs, co
        self.owns, self.gots = scratch[:n], scratch[n:2 * n]
        self.acc = scratch[2 * n]
        bufs = scratch[2 * n + 1:2 * n + 26]
        self.last, send, recv, csend, crecv, self.local = scratch[2 * n + 26:]
        self.sems, self.core = Sems(send, recv), Sems(csend, crecv)
        self.rs = ReduceScatter(self.acc, bufs, self.sems, co, "yl")

    def begin(self):
        co = self.co
        self.cores, self.loads = [], []
        for i, kind in enumerate(self.kinds):
            rows = slab_shape(kind)[0]
            for yl in range(2):
                other = pl.multiple_of((yl * 2 + 1 - co["c"]) * rows, 16)
                self.cores.append(
                    self.core.copy(
                        self.slabs[i].at[pl.ds(other, rows)],
                        self.gots[i].at[yl],
                        partner(co, "core"),
                    )
                )
                mine = pl.multiple_of((yl * 2 + co["c"]) * rows, 16)
                cp = pltpu.make_async_copy(
                    self.slabs[i].at[pl.ds(mine, rows)],
                    self.owns[i].at[yl],
                    self.local.at[2 * i + yl],
                )
                cp.start()
                self.loads.append(cp)

    def fold(self):
        for i, kind in enumerate(self.kinds):
            for yl in range(2):
                self.loads[2 * i + yl].wait()
                self.cores[2 * i + yl].wait_recv()

                def step(p, carry):
                    for x in range(4):
                        for z in range(4):
                            self.acc[yl, x, z, p, i] = fold_block(
                                self.owns[i], self.gots[i], yl, x, z, p, kind
                            )
                    return carry

                lax.fori_loop(0, 5, step, 0)
        for part in range(5):
            self.rs.start(part, 0)

    def stage(self, stage):
        for part in range(5):
            self.rs.finish(part, stage)
            if stage < 4:
                self.rs.start(part, stage + 1)

    def halve(self):
        co = self.co
        theirs = pl.ds(pl.multiple_of((1 - co["yh"]) * 32, 32), 32)
        self.half = self.sems.copy(
            self.acc.at[co["yl"], co["x"], co["z"], :, :, theirs, :],
            self.last,
            partner(co, "y2"),
        )

    def result(self, p):
        co = self.co
        mine = pl.ds(pl.multiple_of(co["yh"] * 32, 32), 32)
        own = self.acc[co["yl"], co["x"], co["z"], p, :, mine, :]
        return (own.astype(F32) + self.last[p].astype(F32)).astype(BF16)

    def drain(self):
        self.half.wait_send()
        self.rs.drain()
        for cp in self.cores:
            cp.wait_send()


MLP = (WIDE, WIDE, TALL)


def backward_kernel(
    kv_ref, w_ref, wt_ref, bias_ref, m_ref, delta_ref, gate_ref, up_ref, down_ref,
    dq_ref, own_ref, mlp_ref, acc, *rest,
):
    bufs, (send, recv) = rest[:25], rest[25:27]
    co = coords()
    greet(co, GRAD_DIMS)
    mlp = GradSum(MLP, (gate_ref, up_ref, down_ref), rest[27:], co)
    mlp.begin()
    rs = ReduceScatter(acc, bufs, Sems(send, recv), co, "y2")
    for g in range(KEY_VALUE_HEADS):
        w, wt = w_ref[g], wt_ref[g]
        top, delta = m_ref[g], delta_ref[g]

        def step(i, dq):
            kv = kv_ref[i // 4, i % 4, :, g].reshape(CHUNK, 128)
            both = jnp.dot(kv, w, preferred_element_type=F32)
            b = bias_ref[pl.ds(i * CHUNK, CHUNK)]
            s = both[:, :ROWS3] + jnp.concatenate([b, b, b], axis=1)
            e = jnp.exp(s - top)
            ds = (e * (both[:, ROWS3:] - delta)).astype(BF16)
            pair = jnp.concatenate([ds, e.astype(BF16)], axis=1)
            dkv = jnp.dot(pair, wt, preferred_element_type=F32)
            acc[i // 4, i % 4, :, g] = dkv.astype(BF16).reshape(4, 128, 128)
            return dq + over_dim0(kv, ds)

        dq_ref[g] = lax.fori_loop(0, 8, step, jnp.zeros((128, ROWS3), F32))
        if g == 1:
            mlp.fold()
        if g == 3:
            mlp.stage(0)
        rs.start(g, 0)
    mlp.stage(1)
    for part in range(5):
        rs.finish(part, 0)
        rs.start(part, 1)
    mlp.stage(2)
    for part in range(5):
        rs.finish(part, 1)
        rs.start(part, 2)
    mlp.stage(3)
    for part in range(5):
        rs.finish(part, 2)
        rs.start(part, 3)
    mlp.stage(4)
    mlp.halve()
    for part in range(5):
        rs.finish(part, 3)
        rs.start(part, 4)
    mlp.half.wait_recv()
    for p in range(5):
        mlp_ref[p] = mlp.result(p)
    for part in range(5):
        rs.finish(part, 4)
    own_ref[...] = acc[co["yh"], co["x"], co["z"]]
    rs.drain()
    mlp.drain()


def backward_call(kv, w, wt, bias, m, delta, gate, up, down):
    shape = jax.ShapeDtypeStruct
    return pl.pallas_call(
        backward_kernel,
        out_shape=(
            shape((5, 128, ROWS3), F32),
            shape((5, 128, 128), BF16),
            shape((5, 3, 32, 128), BF16),
        ),
        in_specs=[INV] * 6 + [ANY] * 3,
        out_specs=[INV] * 3,
        scratch_shapes=[pltpu.VMEM((2, 4, 4, 5, 128, 128), BF16)]
        + [pltpu.VMEM(s, BF16) for s in rs_shapes("y2", (128, 128))]
        + [dma_sems(64), dma_sems(64)]
        + grad_scratch(MLP),
        compiler_params=params(3),
        name="attention_backward",
    )(kv, w, wt, bias, m, delta, gate, up, down)


LAST = (GAIN,)


def last_kernel(slab_ref, mlp_ref, out_ref, mlp_out, *rest):
    msend, mrecv, send, recv = rest[:4]
    co = coords()
    greet(co, GRAD_DIMS)
    here = (co["yh"], co["x"], co["z"])
    grad = GradSum(LAST, (slab_ref,), rest[4:], co)
    grad.begin()
    mlp_out[here] = mlp_ref[...]
    mlp = AllGather(mlp_out, Sems(msend, mrecv), co)
    for part in range(5):
        mlp.start(part, 0)

    def mlp_stage(stage):
        for part in range(5):
            mlp.finish(part, stage)
            if stage < 4:
                mlp.start(part, stage + 1)

    grad.fold()
    mlp_stage(0)
    for stage in range(5):
        grad.stage(stage)
        if stage < 4:
            mlp_stage(stage + 1)
    grad.halve()
    grad.half.wait_recv()
    for p in range(5):
        out_ref[here + (p,)] = grad.result(p)
    ag = AllGather(out_ref, Sems(send, recv), co)
    for part in range(5):
        ag.start(part, 0)
    for stage in range(5):
        for part in range(5):
            ag.finish(part, stage)
            if stage < 4:
                ag.start(part, stage + 1)
    grad.drain()
    mlp.drain()
    ag.drain()


def last_call(slab, mlp):
    shape = jax.ShapeDtypeStruct
    return pl.pallas_call(
        last_kernel,
        out_shape=(
            shape((2, 4, 4, 5, 1, 32, 128), BF16),
            shape((2, 4, 4, 5, 3, 32, 128), BF16),
        ),
        in_specs=[ANY, INV],
        out_specs=[INV, INV],
        scratch_shapes=[dma_sems(48)] * 4 + grad_scratch(LAST),
        compiler_params=params(4),
        name="last_gradients",
    )(slab, mlp)


def unpack_kernel(kinds, first, second, *outs):
    for i, kind in enumerate(kinds):
        src, j = (first, i) if i < len(LAST) else (second, i - len(LAST))

        def part(p, carry):
            for x in range(4):
                for z in range(4):
                    for yh in range(2):
                        block = src[yh, x, z, p, j].astype(F32)
                        if kind != TALL:
                            rows = min(32, kind - 64 * x - 32 * yh)
                            lanes = pl.ds(pl.multiple_of(512 * p + 128 * z, 128), 128)
                            outs[i][pl.ds(64 * x + 32 * yh, rows), lanes] = block[:rows]
                        else:
                            at = 256 * z + 128 * yh
                            count = min(128, 960 - at)
                            rows = pl.ds(pl.multiple_of(128 * p + 32 * x, 8), 32)
                            outs[i][rows, pl.ds(at, count)] = block[:, :count]
            return carry

        lax.fori_loop(0, 5, part, 0)


def unpack_call(first, second):
    kinds = LAST + MLP
    return pl.pallas_call(
        functools.partial(unpack_kernel, kinds),
        out_shape=tuple(jax.ShapeDtypeStruct(slab_shape(kind), F32) for kind in kinds),
        in_specs=[INV, INV],
        out_specs=[INV] * len(kinds),
        compiler_params=pltpu.CompilerParams(vmem_limit_bytes=VMEM_LIMIT),
        name="unpack",
    )(first, second)


def rotation(position_list):
    half_size = HEAD_SIZE // 2
    frequency = 100000.0 ** (-(jnp.arange(half_size, dtype=F32) * 2.0 / HEAD_SIZE))
    angles = position_list.astype(F32)[:, None] * frequency[None, :]
    return jnp.cos(angles)[:, None, :], jnp.sin(angles)[:, None, :]


def apply_rotary(values, turn, head_count, backward):
    half_size = HEAD_SIZE // 2
    cosine, sine = turn
    if backward:
        sine = -sine
    shaped = values.reshape(values.shape[0], head_count, HEAD_SIZE)
    first = shaped[..., :half_size]
    second = shaped[..., half_size:]
    turned = jnp.concatenate(
        [first * cosine - second * sine, second * cosine + first * sine], axis=-1
    )
    return turned.reshape(values.shape[0], head_count * HEAD_SIZE)


def rms_inverse(rows_in):
    return lax.rsqrt(jnp.mean(rows_in * rows_in, axis=-1) + 1e-05)


def norm_back(grad_normed, inputs, inverse, gain_row):
    gain_grad = jnp.sum(grad_normed * inputs * inverse[:, None], axis=0)
    scaled = grad_normed * gain_row
    input_grad = inverse[:, None] * scaled - inputs * (inverse**3)[:, None] * jnp.mean(
        scaled * inputs, axis=-1, keepdims=True
    )
    return (input_grad, gain_grad)


def matrix_product(left, right):
    return jnp.dot(left, right, preferred_element_type=F32)


def by_group(rows):
    t = rows.shape[0]
    return (
        rows.reshape(t, KEY_VALUE_HEADS, QUERY_PER_KV, HEAD_SIZE)
        .transpose(1, 2, 0, 3)
        .reshape(KEY_VALUE_HEADS, ROWS3, HEAD_SIZE)
    )


def shards(
    tokens, positions, w_query, key_weight, value_weight, w_output, gain_attn,
    w_gate, w_up, w_down, gain_mlp, cotangent,
):
    t = tokens.shape[1]
    owned_positions = positions[0]
    w_one = jnp.concatenate([w_query, key_weight, value_weight], axis=1)
    gains = jnp.pad(jnp.stack([gain_attn, gain_mlp]), ((0, 14), (0, 16)))
    w_qkv, gains_all, pos_all = first_call(
        w_one, gains, jnp.broadcast_to(owned_positions[None], (8, 128))
    )
    gains_all = gains_all.reshape(4, 16, 256)[:, :2, :240].astype(F32)
    gain_one = gains_all[:, 0].reshape(960)
    gain_two = gains_all[:, 1].reshape(960)
    full_places = pos_all[:, 0, :].reshape(4096)
    bias = jnp.where(
        owned_positions[None, :] >= full_places[:, None], 0.0, -1e30
    ).astype(F32)

    inputs = tokens[0].astype(F32)
    inverse_one = rms_inverse(inputs)
    normed_one = (inputs * inverse_one[:, None] * gain_one).astype(BF16)
    qkv = matrix_product(normed_one, w_qkv)
    turn = rotation(owned_positions)
    queries = apply_rotary(qkv[:, :960], turn, HQ, False).astype(BF16)
    keys = apply_rotary(qkv[:, 960:1280], turn, KEY_VALUE_HEADS, False).astype(BF16)
    values = qkv[:, 1280:].astype(BF16)
    kv_own = jnp.concatenate(
        [keys.reshape(t, 5, 64), values.reshape(t, 5, 64)], axis=-1
    ).transpose(1, 0, 2)
    q_rows = by_group(queries * BF16(0.125))
    q_turned = q_rows.transpose(0, 2, 1)
    qt = jnp.concatenate([q_turned, jnp.zeros_like(q_turned)], axis=1)

    kv_all, u_all, top, total, wo_all, wg_all, wu_all, wd_all = forward_call(
        kv_own, qt, bias, w_output, w_gate, w_up, w_down
    )
    attended = u_all[:, 64:] / total
    attended_rows = (
        attended.reshape(5, 64, 3, t).transpose(3, 0, 2, 1).reshape(t, 960).astype(BF16)
    )
    middle = inputs + matrix_product(attended_rows, wo_all)
    inverse_two = rms_inverse(middle)
    normed_two = (middle * inverse_two[:, None] * gain_two).astype(BF16)
    gate = matrix_product(normed_two, wg_all)
    upper = matrix_product(normed_two, wu_all)
    sigma = jax.nn.sigmoid(gate)
    hidden = (gate * sigma * upper).astype(BF16)
    result = (middle + matrix_product(hidden, wd_all)).astype(BF16)[None]

    grad_low = cotangent[0]
    grad_out = grad_low.astype(F32)
    term_down = matrix_product(hidden.T, grad_low).astype(BF16)
    grad_hidden = matrix_product(grad_low, wd_all.T)
    grad_gate_low = (grad_hidden * upper * sigma * (1.0 + gate * (1.0 - sigma))).astype(BF16)
    grad_upper_low = (grad_hidden * gate * sigma).astype(BF16)
    term_gate = matrix_product(normed_two.T, grad_gate_low).astype(BF16)
    term_up = matrix_product(normed_two.T, grad_upper_low).astype(BF16)
    grad_normed_two = matrix_product(grad_gate_low, wg_all.T) + matrix_product(
        grad_upper_low, wu_all.T
    )
    norm_grad_two, term_gain_two = norm_back(grad_normed_two, middle, inverse_two, gain_two)
    grad_middle = grad_out + norm_grad_two
    branch_gradient = grad_middle.astype(BF16)
    term_output = matrix_product(attended_rows.T, branch_gradient).astype(BF16)
    grad_attended = (
        matrix_product(branch_gradient, wo_all.T)
        .reshape(t, 5, 3, 64)
        .transpose(1, 3, 2, 0)
        .reshape(5, 64, ROWS3)
    )
    du_turned = (grad_attended / total).astype(BF16)
    delta = jnp.sum(grad_attended * attended, axis=1, keepdims=True) / total
    w_back = jnp.concatenate(
        [
            jnp.concatenate([q_turned, jnp.zeros_like(q_turned)], axis=2),
            jnp.concatenate([jnp.zeros_like(du_turned), du_turned], axis=2),
        ],
        axis=1,
    )
    dq_turned, own_pairs, mlp_own = backward_call(
        kv_all, w_back, w_back.transpose(0, 2, 1), bias, top, delta,
        term_gate, term_up, term_down,
    )
    query_rows = (
        (dq_turned[:, :64] * 0.125)
        .reshape(5, 64, 3, t)
        .transpose(3, 0, 2, 1)
        .reshape(t, 960)
    )
    pairs = own_pairs.transpose(1, 0, 2)
    grad_query_low = apply_rotary(query_rows, turn, HQ, True).astype(BF16)
    grad_key_low = apply_rotary(
        pairs[..., :64].reshape(t, 320).astype(F32), turn, KEY_VALUE_HEADS, True
    ).astype(BF16)
    grad_value_low = pairs[..., 64:].reshape(t, 320)
    grad_qkv = jnp.concatenate([grad_query_low, grad_key_low, grad_value_low], axis=1)
    term_qkv = matrix_product(normed_one.T, grad_qkv).astype(BF16)
    grad_normed_one = matrix_product(grad_qkv, w_qkv.T)
    norm_grad_one, term_gain_one = norm_back(grad_normed_one, inputs, inverse_one, gain_one)
    grad_input = (grad_middle + norm_grad_one).astype(BF16)[None]

    term_gains = jnp.stack([term_gain_one, term_gain_two]).astype(BF16)
    gain_rows = jnp.pad(
        term_gains.reshape(2, 4, 240).transpose(1, 0, 2), ((0, 0), (0, 14), (0, 2320))
    )
    slab = jnp.concatenate(
        [jnp.concatenate([term_qkv, term_output], axis=1).reshape(4, 240, 2560), gain_rows],
        axis=1,
    ).reshape(1024, 2560)
    first, sum_gate, sum_up, sum_down = unpack_call(*last_call(slab, mlp_own))
    return (
        result, grad_input,
        first[:240, :960], first[:240, 960:1280], first[:240, 1280:1600], first[:240, 1600:],
        first[240, :240], sum_gate, sum_up, sum_down, first[241, :240],
    )


def solution(mesh):
    in_specs = (
        P("dp", "ctx", None), P("dp", "ctx"),
        P("dp", None), P("dp", None), P("dp", None), P("dp", None), P("dp"),
        P("dp", None), P("dp", None), P("dp", None), P("dp"),
        P("dp", "ctx", None),
    )
    out_specs = (
        P("dp", "ctx", None), P("dp", "ctx", None),
        P("dp", None), P("dp", None), P("dp", None), P("dp", None), P("dp"),
        P("dp", None), P("dp", None), P("dp", None), P("dp"),
    )
    return jax.shard_map(shards, mesh=mesh, in_specs=in_specs, out_specs=out_specs, check_vma=False)
```

profile of v0, /device:TPU:0, one launch (start us, length us, event | category | flops | bytes accessed | tf_op | source)
XLA Modules:
  0.0 361.0 jit_solution(745862035115973173)
XLA Ops:
  2.8 2.0 concatenate.44.w_ref
  8.0 24.5 %gather_first.1 = (bf16[960,1600]{1,0:T(8,128)(2,1)}, bf16[64,256]{1,0:T(8,128)(2,1)}, s32[32,8,128]{2,1,0:T(8,128)}) custom-call(bf16[240,1600]{1,0:T(8,128)(2,1)} %concatenate.44.w_ref, bf16[16,256]{1,0:T(8,128)(2,1)} %fusion.35.gain_ref, s32[8,128]{1,0:T(8,128)} %broadcast_in_dim.19.pos_ref), custom_call_target="tpu_custom_call" | custom-call | tf_op jit(solution)/shard_map/gather_first/pallas_call | solution.py:406
  34.0 3.5 fusion.28
  41.8 2.9 compare_select_fusion.bias_ref
  44.7 1.9 copy.72.wd_ref
  46.6 70.3 %attention_forward.1 = (bf16[2,4,4,5,128,128]{5,4,3,2,1,0:T(8,128)(2,1)}, f32[5,128,384]{2,1,0:T(8,128)}, f32[5,1,384]{2,1,0:T(1,128)}, f32[5,1,384]{2,1,0:T(1,1...) custom-call(bf16[5,128,128]{2,1,0:T(8,128)(2,1)} %maximum_bitcast_fu, ...), custom_call_target="tpu_custom_call" | custom-call | tf_op jit(solution)/shard_map/attention_forward/pallas_call | solution.py:497
  117.6 1.5 copy.73
  120.0 2.4 multiply_reduce_fusion.2
  122.7 3.4 fusion.44
  127.5 5.3 %multiply_convert_fusion = (bf16[128,2560]{1,0:T(8,128)(2,1)S(1)}, bf16[128,2560]{1,0:T(8,128)(2,1)S(1)}, bf16[128,2560]{1,0:T(8,128)(2,1)S(1)}) fusion(f32[128,2560]{1,0:T(8,128)S(1)} %fusion.44, f32[128,2560]{1,0:T(8,128)S(1)} %fusion.45, bf16[2560,960]{1,0:T(8,128)(2,1)} %get-tuple-element.39, bf16[1,128,960]{1,2,0:T(8,128)(2,1)S(1)} %copy-done.9), kind=kOutput, calls=%fused_computation.15 | convolution fusion | flops 634388480 | bytes 9748480 | tf_op jit(solution)/shard_map/dot_general | solution.py:861
  132.8 2.5 fusion.5
  135.3 1.4 fusion.46
  136.8 2.1 multiply_reduce_fusion
  141.8 2.7 fusion.8
  144.5 1.4 fusion.39
  145.8 1.5 copy.77.w_ref
  147.3 1.3 reshape_divide_fusion.delta_ref
  148.6 4.8 %convolution_convert_fusion.2.gate_ref = bf16[960,2560]{1,0:T(8,128)(2,1)} fusion(bf16[128,960]{0,1:T(8,128)(2,1)S(1)} %multiply_convert_fusion.3, bf16[128,2560]{1,0:T(8,128)(2,1)} %copy-done.5), kind=kOutput, calls=%fused_computation.4 | convolution fusion | flops 631603200 | bytes 5816320 | tf_op jit(solution)/shard_map/dot_general | solution.py:861
  153.5 3.6 convolution_convert_fusion.1.up_ref
  157.1 3.7 %convolution_convert_fusion = bf16[2560,960]{0,1:T(8,128)(2,1)} fusion(bf16[128,2560]{1,0:T(8,128)(2,1)S(1)} %copy-done.4, bf16[1,128,960]{1,2,0:T(8,128)(2,1)S(1)} %copy-done.9), kind=kOutput, calls=%fused_computation.2 | convolution fusion | flops 631603200 | bytes 5816320 | tf_op jit(solution)/shard_map/dot_general | solution.py:861
  160.7 7.9 %copy.78.down_ref = bf16[2560,960]{1,0:T(8,128)(2,1)} copy(bf16[2560,960]{0,1:T(8,128)(2,1)} %convolution_convert_fusion) | data formatting | bytes 9830400 | tf_op jit(solution)/shard_map/convert_element_type | solution.py:925
  168.6 91.3 %attention_backward.1 = (f32[5,128,384]{2,1,0:T(8,128)}, bf16[5,128,128]{2,1,0:T(8,128)(2,1)}, bf16[5,3,32,128]{3,2,1,0:T(8,128)(2,1)}) custom-call(bf16[2,4,4,5,128,128]{5,4,3,2,1,0:T(8,128)(2,1)} %get-tuple-element.40.kv_ref, bf16[5,128,768]{2,1,0:T(8,128)(2,1)} %copy.77.w_ref, bf16[5,768,128]{2,1,0:T(8,128)(2,1)} %get-tuple-element.101.wt_ref, ...), custom_call_target="tpu_custom_call" | custom-call | tf_op jit(solution)/shard_map/attention_backward/pallas_call | solution.py:713
  262.3 3.0 fusion.18
  268.2 1.4 pad_maximum_fusion
  269.5 2.8 fusion.1
  272.4 69.5 %last_gradients.1 = (bf16[2,4,4,5,1,32,128]{6,5,4,3,2,1,0:T(8,128)(2,1)}, bf16[2,4,4,5,3,32,128]{6,5,4,3,2,1,0:T(8,128)(2,1)}) custom-call(bf16[1024,2560]{1,0:T(8,128)(2,1)} %bitcast.92, bf16[5,3,32,128]{3,2,1,0:T(8,128)(2,1)} %get-tuple-element.44.mlp_ref), custom_call_target="tpu_custom_call" | custom-call | tf_op jit(solution)/shard_map/last_gradients/pallas_call | solution.py:777
  341.9 7.2 %unpack.1 = (f32[256,2560]{1,0:T(8,128)}, f32[240,2560]{1,0:T(8,128)}, f32[240,2560]{1,0:T(8,128)}, f32[640,960]{1,0:T(8,128)}) custom-call(bf16[2,4,4,5,1,32,128]{6,5,4,3,2,1,0:T(8,128)(2,1)} %get-tuple-element.45.first, bf16[2,4,4,5,3,32,128]{6,5,4,3,2,1,0:T(8,128)(2,1)} %get-tuple-element.46.second), custom_call_target="tpu_custom_call" | custom-call | tf_op jit(solution)/shard_map/unpack/pallas_call | solution.py:816
  349.1 3.3 fusion.41
  352.4 2.0 fusion.42
  354.4 1.9 copy.84
  357.2 1.3 fusion.40
  358.5 2.0 copy.86
  (110 shorter events, 23.0 us)
Async XLA Ops:
  0.6 32.7 %copy-start.1 = (bf16[1,128,960]{1,2,0:T(8,128)(2,1)S(1)}, bf16[1,128,960]{1,2,0:T(8,128)(2,1)}, u32[]{:S(2)}) copy-start(bf16[1,128,960]{1,2,0:T(8,128)(2,1)} %param.12) | copy-start | bytes 737284
  33.3 4.8 %copy-start.17 = (s32[1,128]{1,0:T(1,128)S(1)}, s32[1,128]{1,0:T(1,128)}, u32[]{:S(2)}) copy-start(s32[1,128]{1,0:T(1,128)} %param.13) | copy-start | bytes 1540
  34.0 4.5 %copy-start.14 = (f32[128]{0:T(128)}, f32[128]{0:T(128)S(1)}, u32[]{:S(2)}) copy-start(f32[128]{0:T(128)S(1)} %get-tuple-element.119) | copy-start | bytes 1540
  39.4 5.4 %copy-start.10 = (bf16[640,960]{0,1:T(8,128)(2,1)S(1)}, bf16[640,960]{0,1:T(8,128)(2,1)}, u32[]{:S(2)}) copy-start(bf16[640,960]{0,1:T(8,128)(2,1)} %param.21) | copy-start | bytes 3686404
  122.5 14.3 %copy-start.12 = (f32[960]{0:T(1024)}, f32[960]{0:T(1024)S(1)}, u32[]{:S(2)}) copy-start(f32[960]{0:T(1024)S(1)} %mul.326) | copy-start | bytes 11524
  122.7 3.9 %copy-start = (bf16[960,2560]{1,0:T(8,128)(2,1)S(1)}, bf16[960,2560]{1,0:T(8,128)(2,1)}, u32[]{:S(2)}) copy-start(bf16[960,2560]{1,0:T(8,128)(2,1)} %get-tuple-element.38) | copy-start | bytes 14745604
  122.7 4.7 %copy-start.9 = (bf16[1,128,960]{1,2,0:T(8,128)(2,1)S(1)}, bf16[1,128,960]{1,2,0:T(8,128)(2,1)}, u32[]{:S(2)}) copy-start(bf16[1,128,960]{1,2,0:T(8,128)(2,1)} %param.23) | copy-start | bytes 737284
  126.5 6.2 %slice-start.2 = ((s8[5242880]{0:T(1024)(128)(4,1)}), s8[4194304]{0:T(1024)(128)(4,1)S(1)}, s32[]{:S(2)}) async-start(s8[5242880]{0:T(1024)(128)(4,1)} %bitcast.96), calls=%async_computation.2 | async-start | bytes 8388608
  126.6 8.7 %slice-start = ((s8[4915200]{0:T(1024)(128)(4,1)}), s8[4194304]{0:T(1024)(128)(4,1)S(1)}, s32[]{:S(2)}) async-start(s8[4915200]{0:T(1024)(128)(4,1)} %bitcast.93), calls=%async_computation | async-start | bytes 8388608
  127.4 5.3 %slice-start.3 = ((s8[5242880]{0:T(1024)(128)(4,1)}), s8[1048576]{0:T(1024)(128)(4,1)S(1)}, s32[]{:S(2)}) async-start(s8[5242880]{0:T(1024)(128)(4,1)} %bitcast.96), calls=%async_computation.3 | async-start | bytes 2097152
  127.5 7.8 %slice-start.1 = ((s8[4915200]{0:T(1024)(128)(4,1)}), s8[720896]{0:T(1024)(128)(4,1)S(1)}, s32[]{:S(2)}) async-start(s8[4915200]{0:T(1024)(128)(4,1)} %bitcast.93), calls=%async_computation.1 | async-start | bytes 1441792
  132.7 2.6 copy-start.3
  132.7 2.6 copy-start.5
  132.7 4.0 %copy-start.6 = (bf16[128,2560]{1,0:T(8,128)(2,1)}, bf16[128,2560]{1,0:T(8,128)(2,1)S(1)}, u32[]{:S(2)}) copy-start(bf16[128,2560]{1,0:T(8,128)(2,1)S(1)} %get-tuple-element.96) | copy-start | bytes 1966084
  136.8 3.1 copy-start.2
  144.5 2.9 copy-start.13
  148.6 4.8 %copy-start.7 = (bf16[128,2560]{1,0:T(8,128)(2,1)S(1)}, bf16[128,2560]{1,0:T(8,128)(2,1)}, u32[]{:S(2)}) copy-start(bf16[128,2560]{1,0:T(8,128)(2,1)} %copy-done.6) | copy-start | bytes 1966084
  153.5 3.6 copy-start.4
  259.9 1.9 copy-start.11
  261.4 0.9 copy-start.15
  262.3 3.1 copy-start.18
  262.3 4.0 %copy-start.16 = (bf16[960]{0:T(1024)(128)(2,1)S(1)}, bf16[960]{0:T(1024)(128)(2,1)}, u32[]{:S(2)}) copy-start(bf16[960]{0:T(1024)(128)(2,1)} %get-tuple-element.84) | copy-start | bytes 5764
  349.1 9.4 %copy-start.8 = (f32[640,960]{1,0:T(8,128)S(1)}, f32[640,960]{1,0:T(8,128)}, u32[]{:S(2)}) copy-start(f32[640,960]{1,0:T(8,128)} %get-tuple-element.82) | copy-start | bytes 7372804
where the time goes:
time: 368 us; the launch traced here: 361 us
  Pallas kernels  263 us (71%)
  matrix products  39.1 us (11%)
  local copies, waits for them, and re-layouts  37.6 us (10%)
  other arithmetic  19.9 us (5%)
    pallas_call x1, Pallas kernels, backward_call(): pl.pallas_call(backward_kernel, out_shape=(shape((5, 128, ROWS3), F32), s...  91.3 us
    pallas_call x1, Pallas kernels, forward_call(): pl.pallas_call(forward_kernel, out_shape=(shape((2, 4, 4, 5, 128, 128), B...  70.3 us
    pallas_call x1, Pallas kernels, last_call(): pl.pallas_call(last_kernel, out_shape=(shape((2, 4, 4, 5, 1, 32, 128), BF...  69.5 us
    dot_general x15, matrix products, matrix_product(): return jnp.dot(left, right, preferred_element_type=F32)  39.1 us
    pallas_call x1, Pallas kernels, first_call(): pl.pallas_call(first_kernel, out_shape=(jax.ShapeDtypeStruct((960, 1600),...  24.5 us
    unnamed x57, local copies, waits for them, and re-layouts  10.6 us
    convert_element_type x1, local copies, waits for them, and re-layouts, shards(): term_down = matrix_product(hidden.T, grad_low).astype(BF16)  7.88 us

commit v1 on v0

v1 whole, which is shorter than its diff:
```python
import jax
import jax.numpy as jnp
from jax import lax
from jax.experimental import pallas as pl
from jax.experimental.pallas import tpu as pltpu
from jax.sharding import PartitionSpec as P

HQ = 15
KEY_VALUE_HEADS = 5
HEAD_SIZE = 64
QUERY_PER_KV = 3
MESH = pl.DeviceIdType.MESH
VMEM_LIMIT = 60 * 2**20
F32 = jnp.float32
BF16 = jnp.bfloat16
ROWS3 = 384


def coords():
    dp = lax.axis_index("dp")
    ctx = lax.axis_index("ctx")
    return dict(yl=dp // 2, c=dp % 2, yh=ctx // 16, x=(ctx // 4) % 4, z=ctx % 4)


def flip(t):
    return t + 1 - 2 * (t % 2)


def partner(co, d):
    new = dict(co)
    if d == "core":
        new["c"] = 1 - co["c"]
    elif d == "x1":
        new["x"] = flip(co["x"])
    elif d == "x3":
        new["x"] = 3 - co["x"]
    elif d == "z1":
        new["z"] = flip(co["z"])
    elif d == "z3":
        new["z"] = 3 - co["z"]
    else:
        if d in ("y1", "y3"):
            new["yl"] = 1 - co["yl"]
        if d in ("y2", "y3"):
            new["yh"] = 1 - co["yh"]
    return new


def device(co):
    return (co["yl"] * 2 + co["c"], co["yh"] * 16 + co["x"] * 4 + co["z"])


def spans(state, t):
    if state == "all":
        return [(0, 4)]
    if state == "both":
        return [(0, 2)]
    if state == "pair":
        return [(t - t % 2, 2)]
    if state == "anti":
        return [(t, 1), (3 - t, 1)]
    return [(t, 1)]


WIDTH = {"all": 4, "both": 2, "pair": 2, "anti": 2, "one": 1}


def less(state, d):
    new = dict(state)
    axis = d[0]
    if axis == "y":
        new["y"] = "one"
    elif state[axis] == "all":
        new[axis] = "anti" if d[1] == "1" else "pair"
    else:
        new[axis] = "one"
    return new


def more(state, d):
    new = dict(state)
    axis = d[0]
    if axis == "y":
        new["y"] = "both"
    elif state[axis] == "one":
        new[axis] = "pair" if d[1] == "1" else "anti"
    else:
        new[axis] = "all"
    return new


def boxes(state, co, ykey):
    out = []
    place_y = 0
    for ys, yn in spans(state["y"], co[ykey]):
        place_x = 0
        for xs, xn in spans(state["x"], co["x"]):
            place_z = 0
            for zs, zn in spans(state["z"], co["z"]):
                out.append(
                    (
                        (pl.ds(ys, yn), pl.ds(xs, xn), pl.ds(zs, zn)),
                        (pl.ds(place_y, yn), pl.ds(place_x, xn), pl.ds(place_z, zn)),
                        (yn, xn, zn),
                    )
                )
                place_z += zn
            place_x += xn
        place_y += yn
    return out


FULL = dict(y="both", x="all", z="all")
SINGLE = dict(y="one", x="one", z="one")


def order(ydim, part):
    dims = ["x1", "x3", "z1", "z3", ydim]
    return dims[part:] + dims[:part]


def rs_states(ydim, part):
    states = []
    state = FULL
    for d in order(ydim, part):
        state = less(state, d)
        states.append(state)
    return states


def rs_shapes(ydim, block):
    return [
        (WIDTH[s["y"]], WIDTH[s["x"]], WIDTH[s["z"]]) + block
        for part in range(5)
        for s in rs_states(ydim, part)
    ]


class Sems:
    def __init__(self, send, recv):
        self.send, self.recv, self.count = send, recv, 0

    def take(self):
        i = self.count
        self.count += 1
        return self.send.at[i], self.recv.at[i]

    def copy(self, src, dst, co):
        s, r = self.take()
        cp = pltpu.make_async_remote_copy(
            src_ref=src, dst_ref=dst, send_sem=s, recv_sem=r,
            device_id=device(co), device_id_type=MESH,
        )
        cp.start()
        return cp


def greet(co, dims):
    barrier = pltpu.get_barrier_semaphore()
    for d in dims:
        pl.semaphore_signal(
            barrier, inc=1, device_id=device(partner(co, d)), device_id_type=MESH
        )
    pl.semaphore_wait(barrier, len(dims))


def add_boxes(pairs, acc, tail, buf, head):
    for box, place, (yn, xn, zn) in pairs:
        (by, bx, bz), (py, px, pz) = box, place

        def add(i, carry):
            iy, ix = i // xn, i % xn
            here = (by.start + iy, bx.start + ix, bz) + tail
            there = head + (py.start + iy, px.start + ix, pz)
            acc[here] = (acc[here].astype(F32) + buf[there].astype(F32)).astype(BF16)
            return carry

        if yn * xn == 1:
            add(0, 0)
        else:
            lax.fori_loop(0, yn * xn, add, 0)


class PlaneReduce:
    DIMS = ["x1", "x3", "z1", "z3"]

    @classmethod
    def plan(cls, part, y):
        dims = (cls.DIMS[part:] + cls.DIMS[:part])[::-1]
        states = []
        state = dict(y=y, x="all", z="all")
        for d in dims:
            state = less(state, d)
            states.append(state)
        return dims, states

    @classmethod
    def shapes(cls, y, lead, block):
        return [
            lead + (WIDTH[y], WIDTH[s["x"]], WIDTH[s["z"]]) + block
            for part in range(4)
            for s in cls.plan(part, y)[1]
        ]

    def __init__(self, acc, bufs, sems, co, y):
        self.acc, self.bufs, self.sems, self.co, self.y = acc, bufs, sems, co, y
        self.ykey = "yh" if y == "both" else "yl"
        self.quarter = acc.shape[-2] // 4
        self.flying, self.sent = {}, []

    def send(self, tail, lead, part, stage):
        dims, states = self.plan(part, self.y)
        to = partner(self.co, dims[stage])
        rows = pl.ds(self.quarter * part, self.quarter)
        buf = self.bufs[part * 4 + stage]
        out = []
        for box, place, _ in boxes(states[stage], to, self.ykey):
            src = self.acc.at[box + tail + (rows,)]
            out.append(self.sems.copy(src, buf.at[lead + place], to))
        self.flying[lead, part] = out
        self.sent += out

    def step(self, tail, lead, stage):
        for part in range(4):
            if stage > 0:
                for cp in self.flying[lead, part]:
                    cp.wait_recv()
                rows = pl.ds(self.quarter * part, self.quarter)
                add_boxes(
                    boxes(self.plan(part, self.y)[1][stage - 1], self.co, self.ykey),
                    self.acc, tail + (rows,), self.bufs[part * 4 + stage - 1], lead,
                )
            if stage < 4:
                self.send(tail, lead, part, stage)

    def drain(self):
        for cp in self.sent:
            cp.wait_send()


class PairSum:
    def __init__(self, acc, own, last, bufs, sems, co):
        self.acc, self.own, self.last, self.sems, self.co = acc, own, last, sems, co
        self.plane = PlaneReduce(acc, bufs, sems, co, "both")
        self.at, self.halves = {}, {}

    def advance(self, g):
        at = self.at[g] = self.at.get(g, -1) + 1
        co = self.co
        if at < 5:
            self.plane.step((g,), (g,), at)
        if at == 4:
            there = (1 - co["yh"], co["x"], co["z"], g)
            self.halves[g] = self.sems.copy(
                self.acc.at[there], self.last.at[g], partner(co, "y2")
            )
        elif at == 5:
            self.halves[g].wait_recv()
            here = (co["yh"], co["x"], co["z"], g)
            self.own[g] = (
                self.acc[here].astype(F32) + self.last[g].astype(F32)
            ).astype(BF16)

    def drain(self):
        self.plane.drain()
        for cp in self.halves.values():
            cp.wait_send()


class ReduceScatter:
    def __init__(self, acc, bufs, sems, co, ydim):
        self.acc, self.bufs, self.sems, self.co, self.ydim = acc, bufs, sems, co, ydim
        self.ykey = "yl" if ydim == "yl" else "yh"
        self.flying = {}
        self.sent = []

    def start(self, part, stage):
        d = order(self.ydim, part)[stage]
        state = rs_states(self.ydim, part)[stage]
        buf = self.bufs[part * 5 + stage]
        out = []
        if d == "yl":
            half = self.acc.shape[-2] // 2
            ways = [("y1", pl.ds(0, half)), ("y3", pl.ds(half, half))]
        else:
            ways = [(d, slice(None))]
        for way, rows in ways:
            to = partner(self.co, way)
            for box, place, _ in boxes(state, to, self.ykey):
                middle = (slice(None),) * (len(self.acc.shape) - 6)
                src = self.acc.at[box + (part,) + middle + (rows, slice(None))]
                dst = buf.at[place + middle + (rows, slice(None))]
                out.append(self.sems.copy(src, dst, to))
        self.flying[part, stage] = out
        self.sent += out

    def finish(self, part, stage):
        for cp in self.flying[part, stage]:
            cp.wait_recv()
        state = rs_states(self.ydim, part)[stage]
        buf = self.bufs[part * 5 + stage]
        add_boxes(
            boxes(state, self.co, self.ykey), self.acc, (part,), buf, ()
        )

    def drain(self):
        for cp in self.sent:
            cp.wait_send()


class AllGather:
    def __init__(self, buf, sems, co, ydim="y2"):
        self.buf, self.sems, self.co, self.ydim = buf, sems, co, ydim
        self.flying = {}
        self.sent = []

    def start(self, part, stage):
        dims = order(self.ydim, part)
        state = SINGLE
        for d in dims[:stage]:
            state = more(state, d)
        to = partner(self.co, dims[stage])
        out = []
        for box, _, _ in boxes(state, self.co, "yh"):
            ref = self.buf.at[box + (part,)]
            out.append(self.sems.copy(ref, ref, to))
        self.flying[part, stage] = out
        self.sent += out

    def finish(self, part, stage):
        for cp in self.flying[part, stage]:
            cp.wait_recv()

    def drain(self):
        for cp in self.sent:
            cp.wait_send()


class PlaneGather:
    DIMS = ["x1", "x3", "z1", "z3"]

    def __init__(self, buf, places, sems, co):
        self.buf, self.places, self.sems, self.co = buf, places, sems, co
        self.flying, self.sent = {}, []

    def first(self):
        co = self.co
        out = []
        for buf in (self.places, self.buf):
            ref = buf.at[co["yh"], co["x"], co["z"]]
            out.append(self.sems.copy(ref, ref, partner(co, "y2")))
        for cp in out:
            cp.wait_recv()
        self.sent += out

    def start(self, part, stage):
        dims = self.DIMS[part:] + self.DIMS[:part]
        state = dict(y="both", x="one", z="one")
        for d in dims[:stage]:
            state = more(state, d)
        to = partner(self.co, dims[stage])
        rows = pl.ds(32 * part, 32)
        for g in range(5) if stage == 3 else [None]:
            out = []
            for box, _, _ in boxes(state, self.co, "yh"):
                if part == 0 and g in (None, 0):
                    ref = self.places.at[box]
                    out.append(self.sems.copy(ref, ref, to))
                ref = self.buf.at[box + (slice(None) if g is None else g, rows)]
                out.append(self.sems.copy(ref, ref, to))
            self.flying[part, stage, g or 0] = out
            self.sent += out

    def finish(self, part, stage, g=0):
        for cp in self.flying[part, stage, g]:
            cp.wait_recv()

    def drain(self):
        for cp in self.sent:
            cp.wait_send()


class Gather:
    def __init__(self, items, sems, local, co):
        self.items, self.sems, self.local, self.co = items, sems, local, co
        self.waits = []

    def block(self, i, q, first, count):
        src, dst, h, lanes = self.items[i]
        n, width = src.shape
        if lanes:
            where = pl.ds(pl.multiple_of(q * width, 128), width)
            return dst.at[pl.ds(first, count), where]
        return dst.at[pl.ds(pl.multiple_of(q * n + first, 16), count)]

    def start(self):
        co = self.co
        me = co["yl"] * 2 + co["c"]
        self.stage = []
        for i, (src, dst, h, lanes) in enumerate(self.items):
            n = src.shape[0]
            one = self.sems.copy(
                src.at[pl.ds(0, h)], self.block(i, me, 0, h), partner(co, "y1")
            )
            two = None
            if h < n:
                two = self.sems.copy(
                    src.at[pl.ds(h, n - h)], self.block(i, me, h, n - h), partner(co, "y3")
                )
            self.stage.append((one, two))
            whole = self.block(i, me, 0, n)
            self.waits.append(self.sems.copy(src, whole, partner(co, "core")))
            cp = pltpu.make_async_copy(src, whole, self.local.at[i])
            cp.start()
            self.waits.append(cp)

    def forward(self, i):
        co = self.co
        src, dst, h, lanes = self.items[i]
        n = src.shape[0]
        q = (1 - co["yl"]) * 2 + co["c"]
        for cp, first, count in zip(self.stage[i], (0, h), (h, n - h)):
            if cp is None:
                continue
            cp.wait_recv()
            ref = self.block(i, q, first, count)
            self.waits.append(self.sems.copy(ref, ref, partner(co, "core")))

    def finish(self):
        for one, two in self.stage:
            one.wait_send()
            if two is not None:
                two.wait_send()
        for cp in self.waits:
            cp.wait()


def params(cid):
    return pltpu.CompilerParams(
        collective_id=cid, has_side_effects=True, vmem_limit_bytes=VMEM_LIMIT
    )


def dma_sems(n):
    return pltpu.SemaphoreType.DMA((n,))


ANY = pl.BlockSpec(memory_space=pl.ANY)
INV = pl.BlockSpec(memory_space=pltpu.VMEM)


def first_kernel(w_ref, gain_ref, w_out, gain_out, send, recv, local):
    co = coords()
    greet(co, ("core", "y1", "y3"))
    gather = Gather(
        [(gain_ref, gain_out, 240, False), (w_ref, w_out, 128, False)],
        Sems(send, recv), local, co,
    )
    gather.start()
    gather.forward(0)
    gather.forward(1)
    gather.finish()


def first_call(w_one, gains):
    return pl.pallas_call(
        first_kernel,
        out_shape=(
            jax.ShapeDtypeStruct((960, 1600), BF16),
            jax.ShapeDtypeStruct((960, 128), BF16),
        ),
        in_specs=[INV] * 2,
        out_specs=[ANY] * 2,
        scratch_shapes=[dma_sems(8), dma_sems(8), dma_sems(3)],
        compiler_params=params(1),
        name="gather_first",
    )(w_one, gains)


CHUNK = 512


def over_lanes(left, right):
    return lax.dot_general(
        left, right, (((1,), (1,)), ((), ())), preferred_element_type=F32
    )


def over_dim0(left, right):
    return lax.dot_general(
        left, right, (((0,), (0,)), ((), ())), preferred_element_type=F32
    )


def forward_kernel(
    kv_ref, qt_ref, pos_ref, wo_ref, wg_ref, wu_ref, wd_ref,
    kv_all, bias_ref, u_ref, m_ref, l_ref, wo_all, wg_all, wu_all, wd_all,
    scores, places, send, recv, wsend, wrecv, local,
):
    co = coords()
    greet(co, ("x1", "x3", "z1", "z3", "y2", "core", "y1", "y3"))
    weights = Gather(
        [
            (wo_ref, wo_all, 128, False),
            (wg_ref, wg_all, 128, False),
            (wu_ref, wu_all, 128, False),
            (wd_ref, wd_all, 480, True),
        ],
        Sems(wsend, wrecv), local, co,
    )
    here = (co["yh"], co["x"], co["z"])
    kv_all[here] = kv_ref[...]
    places[here] = pos_ref[...]
    ag = PlaneGather(kv_all, places, Sems(send, recv), co)
    ag.first()
    for part in range(4):
        ag.start(part, 0)
    weights.start()
    for stage in range(1, 4):
        for part in range(4):
            ag.finish(part, stage - 1)
            ag.start(part, stage)
    for part in range(4):
        ag.finish(part, 3, 0)
    steps = lax.broadcasted_iota(jnp.int32, (64, 128), 0)

    def mask(i, carry):
        row = places[i // 16, (i // 4) % 4, i % 4][0:1]
        for half in range(2):
            ahead = pos_ref[0:1] - row[:, 64 * half:64 * half + 1]
            bias_ref[pl.ds(pl.multiple_of(i * 128 + 64 * half, 64), 64)] = jnp.where(
                steps <= ahead, 0.0, -1e30
            ).astype(F32)
        return carry

    lax.fori_loop(0, 32, mask, 0)

    for g in range(KEY_VALUE_HEADS):
        qt = qt_ref[g]
        if g > 0:
            for part in range(4):
                ag.finish(part, 3, g)
        if g == 4:
            weights.forward(0)
            weights.forward(1)

        def score(i, top):
            kv = kv_all[i // 4, i % 4, :, g].reshape(CHUNK, 128)
            s = jnp.dot(kv, qt, preferred_element_type=F32)
            b = bias_ref[pl.ds(i * CHUNK, CHUNK)]
            s = s + jnp.concatenate([b, b, b], axis=1)
            scores[pl.ds(i * CHUNK, CHUNK)] = s
            return jnp.maximum(top, jnp.max(s.reshape(CHUNK // 8, 8, ROWS3), axis=0))

        top = lax.fori_loop(0, 8, score, jnp.full((8, ROWS3), -1e30, F32))
        top = jnp.max(top, axis=0, keepdims=True)

        def weigh(i, carry):
            total, u = carry
            kv = kv_all[i // 4, i % 4, :, g].reshape(CHUNK, 128)
            e = jnp.exp(scores[pl.ds(i * CHUNK, CHUNK)] - top)
            total = total + jnp.sum(e.reshape(CHUNK // 8, 8, ROWS3), axis=0)
            return total, u + over_dim0(kv, e.astype(BF16))

        carry = (jnp.zeros((8, ROWS3), F32), jnp.zeros((128, ROWS3), F32))
        total, u = lax.fori_loop(0, 8, weigh, carry)
        u_ref[g] = u
        m_ref[g] = top
        l_ref[g] = jnp.sum(total, axis=0, keepdims=True)
    weights.forward(2)
    weights.forward(3)
    ag.drain()
    weights.finish()


def forward_call(kv, qt, pos, wo, wg, wu, wd):
    shape = jax.ShapeDtypeStruct
    return pl.pallas_call(
        forward_kernel,
        out_shape=(
            shape((2, 4, 4, 5, 128, 128), BF16),
            shape((4096, 128), F32),
            shape((5, 128, ROWS3), F32),
            shape((5, 1, ROWS3), F32),
            shape((5, 1, ROWS3), F32),
            shape((960, 960), BF16),
            shape((960, 2560), BF16),
            shape((960, 2560), BF16),
            shape((960, 2560), BF16),
        ),
        in_specs=[INV] * 7,
        out_specs=[INV] * 5 + [ANY] * 4,
        scratch_shapes=[
            pltpu.VMEM((4096, ROWS3), F32),
            pltpu.VMEM((2, 4, 4, 8, 128), jnp.int32),
            dma_sems(128), dma_sems(128), dma_sems(20), dma_sems(20), dma_sems(4),
        ],
        compiler_params=params(2),
        name="attention_forward",
    )(kv, qt, pos, wo, wg, wu, wd)


WIDE, TALL, GAIN = 240, 640, 256


def slab_shape(kind):
    return (960, 640) if kind == TALL else (kind, 2560)


def term(kind, lhs, rhs, q, p):
    if kind == TALL:
        lanes = pl.ds(pl.multiple_of(640 * q + 128 * p, 128), 128)
        return jnp.dot(lhs[...], rhs[:, lanes], preferred_element_type=F32)
    rows = pl.ds(pl.multiple_of(240 * q, 16), 240)
    lanes = pl.ds(pl.multiple_of(512 * p, 128), 512)
    if kind == GAIN:
        return over_lanes(lhs[rows], rhs[lanes])
    return jnp.dot(lhs[rows], rhs[:, lanes], preferred_element_type=F32)


def part_lanes(kind, p):
    width = 128 if kind == TALL else 512
    return pl.ds(pl.multiple_of(width * p, 128), width)


GRAD_DIMS = ("x1", "x3", "z1", "z3", "y1", "y2", "y3", "core")


def grad_scratch(kinds):
    n = len(kinds)
    blocks = [(2,) + slab_shape(kind) for kind in kinds]
    return (
        [pltpu.VMEM(b, BF16) for b in blocks]
        + [pltpu.VMEM(b, BF16) for b in blocks]
        + [pltpu.VMEM((2, 4, 4, 5, n, 64, 128), BF16)]
        + [pltpu.VMEM(s, BF16) for s in rs_shapes("yl", (n, 64, 128))]
        + [pltpu.VMEM((5, n, 32, 128), BF16)]
        + [dma_sems(64), dma_sems(64), dma_sems(2 * n), dma_sems(2 * n)]
    )


def send_terms(kind, factors, gains, out, got, sems, co):
    lhs, rhs = factors
    copies = []
    for yl in range(2):
        q = yl * 2 + 1 - co["c"]

        def step(p, carry):
            value = term(kind, lhs, rhs, q, p).astype(BF16)
            out[yl, pl.ds(0, value.shape[0]), part_lanes(kind, p)] = value
            return carry

        lax.fori_loop(0, 5, step, 0)
        if kind == GAIN:
            out[yl, 240:256, :] = jnp.zeros((16, 2560), BF16)
            rows = pl.ds(pl.multiple_of(16 * q, 16), 16)
            out[yl, 240:256, 0:256] = gains[rows]
        copies.append(sems.copy(out.at[yl], got.at[yl], partner(co, "core")))
    return copies


def fold_terms(kind, factors, gains, got, copies, put, co):
    lhs, rhs = factors
    for yl in range(2):
        q = yl * 2 + co["c"]
        copies[yl].wait_recv()

        def step(p, carry):
            value = term(kind, lhs, rhs, q, p)
            count = value.shape[0]
            value = value + got[yl, pl.ds(0, count), part_lanes(kind, p)].astype(F32)
            value = value.astype(BF16)
            if count % 64:
                pad = jnp.zeros((64 - count % 64, value.shape[1]), BF16)
                value = jnp.concatenate([value, pad], axis=0)
            for x in range(4):
                for z in range(4):
                    if kind == TALL:
                        first = min(256 * x + 64 * z, 896)
                        block = value[first:first + 64]
                    else:
                        block = value[64 * x:64 * x + 64, 128 * z:128 * z + 128]
                    put(yl, x, z, p, block)
            return carry

        lax.fori_loop(0, 5, step, 0)


class GradSum:
    def __init__(self, kinds, factors, gains, scratch, co):
        n = len(kinds)
        self.kinds, self.factors, self.gains, self.co = kinds, factors, gains, co
        self.outs, self.gots = scratch[:n], scratch[n:2 * n]
        self.acc = scratch[2 * n]
        bufs = scratch[2 * n + 1:2 * n + 26]
        self.last, send, recv, csend, crecv = scratch[2 * n + 26:]
        self.sems, self.core = Sems(send, recv), Sems(csend, crecv)
        self.rs = ReduceScatter(self.acc, bufs, self.sems, co, "yl")
        self.cores = []

    def begin(self, i):
        self.cores += send_terms(
            self.kinds[i], self.factors[i], self.gains, self.outs[i], self.gots[i],
            self.core, self.co,
        )

    def fold(self, i):
        co, kind, got = self.co, self.kinds[i], self.gots[i]

        def put(yl, x, z, p, block):
            self.acc[yl, x, z, p, i] = block

        copies = self.cores[2 * i:2 * i + 2]
        fold_terms(kind, self.factors[i], self.gains, got, copies, put, co)
        if kind == GAIN:
            for yl in range(2):
                q = yl * 2 + co["c"]
                rows = pl.ds(pl.multiple_of(16 * q, 16), 16)
                for z in range(2):
                    lanes = slice(128 * z, 128 * z + 128)
                    self.acc[yl, 3, z, 0, i, 48:64, :] = (
                        self.gains[rows, lanes].astype(F32)
                        + got[yl, 240:256, lanes].astype(F32)
                    ).astype(BF16)

    def launch(self):
        for part in range(5):
            self.rs.start(part, 0)

    def stage(self, stage):
        for part in range(5):
            self.rs.finish(part, stage)
            if stage < 4:
                self.rs.start(part, stage + 1)

    def halve(self):
        co = self.co
        theirs = pl.ds(pl.multiple_of((1 - co["yh"]) * 32, 32), 32)
        self.half = self.sems.copy(
            self.acc.at[co["yl"], co["x"], co["z"], :, :, theirs, :],
            self.last,
            partner(co, "y2"),
        )

    def result(self, p):
        co = self.co
        mine = pl.ds(pl.multiple_of(co["yh"] * 32, 32), 32)
        own = self.acc[co["yl"], co["x"], co["z"], p, :, mine, :]
        return (own.astype(F32) + self.last[p].astype(F32)).astype(BF16)

    def drain(self):
        self.half.wait_send()
        self.rs.drain()
        for cp in self.cores:
            cp.wait_send()


class SlabSum:
    def __init__(self, kind, factors, out_ref, i, scratch, co, late):
        self.late = late
        self.kind, self.factors, self.out_ref, self.i, self.co = kind, factors, out_ref, i, co
        self.out, self.got, self.acc, self.ybuf, self.last = scratch[:5]
        send, recv = scratch[21:]
        self.sems = Sems(send, recv)
        y = "both" if late else "one"
        self.plane = PlaneReduce(self.acc, scratch[5:21], self.sems, co, y)
        self.at = 0

    @staticmethod
    def scratch(kind, late):
        return (
            [pltpu.VMEM((2,) + slab_shape(kind), BF16)] * 2
            + [
                pltpu.VMEM((2, 4, 4, 5, 64, 128), BF16),
                pltpu.VMEM((5, 64, 128) if late else (4, 4, 5, 64, 128), BF16),
                pltpu.VMEM((5, 32, 128), BF16),
            ]
            + [pltpu.VMEM(s, BF16) for s in PlaneReduce.shapes("both" if late else "one", (), (5, 16, 128))]
            + [dma_sems(32), dma_sems(32)]
        )

    def begin(self):
        self.cores = send_terms(
            self.kind, self.factors, None, self.out, self.got, self.sems, self.co
        )

    def fold(self):
        def put(yl, x, z, p, block):
            self.acc[yl, x, z, p] = block

        fold_terms(self.kind, self.factors, None, self.got, self.cores, put, self.co)
        if self.late:
            self.plane.step((slice(None),), (), 0)
        else:
            self.send_y()

    def send_y(self):
        co = self.co
        self.halves = []
        for way, first in (("y1", 0), ("y3", 32)):
            if self.late:
                rows = (slice(None), pl.ds(first, 32))
                src = self.acc.at[(1 - co["yl"], co["x"], co["z"]) + rows]
            else:
                rows = (slice(None),) * 3 + (pl.ds(first, 32),)
                src = self.acc.at[(1 - co["yl"],) + rows]
            self.halves.append(self.sems.copy(src, self.ybuf.at[rows], partner(co, way)))

    def add_y(self):
        co = self.co
        yl = co["yl"]
        for cp in self.halves:
            cp.wait_recv()

        def add(here, there):
            self.acc[(yl,) + here] = (
                self.acc[(yl,) + here].astype(F32) + self.ybuf[there].astype(F32)
            ).astype(BF16)

        if self.late:
            add((co["x"], co["z"]), (slice(None),))
        else:

            def step(i, carry):
                add((i // 4, i % 4), (i // 4, i % 4))
                return carry

            lax.fori_loop(0, 16, step, 0)

    def send_half(self):
        co = self.co
        theirs = pl.ds(pl.multiple_of((1 - co["yh"]) * 32, 32), 32)
        src = self.acc.at[co["yl"], co["x"], co["z"], :, theirs, :]
        self.half = self.sems.copy(src, self.last, partner(co, "y2"))

    def advance(self):
        at, co = self.at, self.co
        self.at += 1
        tail = (slice(None),)
        if self.late:
            if at < 4:
                self.plane.step(tail, (), at + 1)
            if at == 3:
                self.send_y()
            if at == 4:
                self.add_y()
                self.send_half()
        else:
            if at == 0:
                self.add_y()
            if at < 5:
                self.plane.step(tail, (), at)
            if at == 4:
                self.send_half()
        if at == 5:
            self.half.wait_recv()
            mine = pl.ds(pl.multiple_of(co["yh"] * 32, 32), 32)
            own = self.acc[co["yl"], co["x"], co["z"], :, mine, :]
            self.out_ref[:, self.i] = (own.astype(F32) + self.last[...].astype(F32)).astype(BF16)

    def drain(self):
        self.plane.drain()
        self.half.wait_send()
        for cp in self.cores + self.halves:
            cp.wait_send()


MLP = (WIDE, WIDE, TALL)
LATE = (True, False, False)


def backward_kernel(
    kv_ref, w_ref, bias_ref, m_ref, delta_ref, h_ref, dg_ref, dp_ref, dy_ref, z_ref,
    dq_ref, own_ref, mlp_ref, acc, last, *rest,
):
    bufs, (send, recv) = rest[:16], rest[16:18]
    co = coords()
    greet(co, GRAD_DIMS)
    factors = ((h_ref, dg_ref), (h_ref, dp_ref), (dy_ref, z_ref))
    slabs, at = [], 18
    for i, kind in enumerate(MLP):
        count = len(SlabSum.scratch(kind, LATE[i]))
        slabs.append(SlabSum(kind, factors[i], mlp_ref, i, rest[at:at + count], co, LATE[i]))
        at += count
    for slab in slabs:
        slab.begin()
    slabs[0].fold()
    slabs[1].fold()
    pairs = PairSum(acc, own_ref, last, bufs, Sems(send, recv), co)
    starts = (2, 3, 5)
    for g in range(KEY_VALUE_HEADS):
        w = w_ref[g]
        top, delta = m_ref[g], delta_ref[g]

        def step(i, dq):
            kv = kv_ref[i // 4, i % 4, :, g].reshape(CHUNK, 128)
            both = jnp.dot(kv, w, preferred_element_type=F32)
            b = bias_ref[pl.ds(i * CHUNK, CHUNK)]
            s = both[:, :ROWS3] + jnp.concatenate([b, b, b], axis=1)
            e = jnp.exp(s - top)
            ds = (e * (both[:, ROWS3:] - delta)).astype(BF16)
            pair = jnp.concatenate([ds, e.astype(BF16)], axis=1)
            dkv = over_lanes(pair, w)
            acc[i // 4, i % 4, :, g] = dkv.astype(BF16).reshape(4, 128, 128)
            return dq + over_dim0(kv, ds)

        dq = jnp.zeros((128, ROWS3), F32)
        for half in range(2):
            dq = lax.fori_loop(4 * half, 4 * half + 4, step, dq)
            if half == 1:
                dq_ref[g] = dq
                pairs.advance(g)
            now = 2 * g + half
            for early in range(g):
                if pairs.at[early] < (5 if now >= 8 else 3):
                    pairs.advance(early)
            if now == 0:
                slabs[2].fold()
            for slab, start in zip(slabs, starts):
                if now >= start and slab.at < 6:
                    slab.advance()
    for turn in range(5):
        for g in (4, 3, 2, 1, 0):
            if pairs.at[g] < 5:
                pairs.advance(g)
        for slab in slabs:
            if slab.at < 6:
                slab.advance()
    pairs.drain()
    for slab in slabs:
        slab.drain()


def backward_call(*args):
    shape = jax.ShapeDtypeStruct
    return pl.pallas_call(
        backward_kernel,
        out_shape=(
            shape((5, 128, ROWS3), F32),
            shape((5, 128, 128), BF16),
            shape((5, 3, 32, 128), BF16),
        ),
        in_specs=[INV] * 10,
        out_specs=[INV] * 3,
        scratch_shapes=[
            pltpu.VMEM((2, 4, 4, 5, 128, 128), BF16),
            pltpu.VMEM((5, 128, 128), BF16),
        ]
        + [pltpu.VMEM(s, BF16) for s in PlaneReduce.shapes("both", (5,), (32, 128))]
        + [dma_sems(128), dma_sems(128)]
        + [s for kind, late in zip(MLP, LATE) for s in SlabSum.scratch(kind, late)],
        compiler_params=params(3),
        name="attention_backward",
    )(*args)


LAST = (GAIN,)


def last_kernel(lhs_ref, rhs_ref, gain_ref, mlp_ref, out_ref, mlp_out, *rest):
    msend, mrecv, send, recv = rest[:4]
    co = coords()
    greet(co, GRAD_DIMS)
    here = (co["yh"], co["x"], co["z"])
    grad = GradSum(LAST, ((lhs_ref, rhs_ref),), gain_ref, rest[4:], co)
    grad.begin(0)
    mlp_out[here] = mlp_ref[...]
    mlp = AllGather(mlp_out, Sems(msend, mrecv), co)
    for part in range(5):
        mlp.start(part, 0)

    def mlp_stage(stage):
        for part in range(5):
            mlp.finish(part, stage)
            if stage < 4:
                mlp.start(part, stage + 1)

    grad.fold(0)
    grad.launch()
    mlp_stage(0)
    for stage in range(5):
        grad.stage(stage)
        if stage < 4:
            mlp_stage(stage + 1)
    grad.halve()
    grad.half.wait_recv()
    for p in range(5):
        out_ref[here + (p,)] = grad.result(p)
    ag = AllGather(out_ref, Sems(send, recv), co)
    for part in range(5):
        ag.start(part, 0)
    for stage in range(5):
        for part in range(5):
            ag.finish(part, stage)
            if stage < 4:
                ag.start(part, stage + 1)
    grad.drain()
    mlp.drain()
    ag.drain()


def last_call(*args):
    shape = jax.ShapeDtypeStruct
    return pl.pallas_call(
        last_kernel,
        out_shape=(
            shape((2, 4, 4, 5, 1, 32, 128), BF16),
            shape((2, 4, 4, 5, 3, 32, 128), BF16),
        ),
        in_specs=[INV] * 4,
        out_specs=[INV, INV],
        scratch_shapes=[dma_sems(48)] * 4 + grad_scratch(LAST),
        compiler_params=params(4),
        name="last_gradients",
    )(*args)


def unpack_kernel(first, second, q_ref, k_ref, v_ref, o_ref, gain_ref, *outs):
    for x in range(4):
        for yh in range(2):
            at = 64 * x + 32 * yh
            value = jnp.concatenate(
                [first[yh, x, z, p, 0].astype(F32) for p in range(5) for z in range(4)], axis=1
            )
            rows = min(32, 240 - at)
            for ref, lane in ((q_ref, 0), (k_ref, 960), (v_ref, 1280), (o_ref, 1600)):
                ref[at:at + rows] = value[:rows, lane:lane + ref.shape[1]]
            if rows < 32:
                gain_ref[...] = value[rows:, :256]
    for i, kind in enumerate(MLP):

        def part(p, carry):
            for x in range(4):
                for z in range(4):
                    for yh in range(2):
                        block = second[yh, x, z, p, i].astype(F32)
                        if kind != TALL:
                            rows = min(32, kind - 64 * x - 32 * yh)
                            lanes = pl.ds(pl.multiple_of(512 * p + 128 * z, 128), 128)
                            outs[i][pl.ds(64 * x + 32 * yh, rows), lanes] = block[:rows]
                        elif x * 4 + z < 15:
                            lanes = pl.ds(pl.multiple_of(128 * p, 128), 128)
                            outs[i][pl.ds(256 * x + 64 * z + 32 * yh, 32), lanes] = block
            return carry

        lax.fori_loop(0, 5, part, 0)


def unpack_call(first, second):
    shapes = [(240, 960), (240, 320), (240, 320), (240, 960), (16, 256)]
    shapes += [slab_shape(kind) for kind in MLP]
    return pl.pallas_call(
        unpack_kernel,
        out_shape=tuple(jax.ShapeDtypeStruct(s, F32) for s in shapes),
        in_specs=[INV, INV],
        out_specs=[INV] * len(shapes),
        compiler_params=pltpu.CompilerParams(vmem_limit_bytes=VMEM_LIMIT),
        name="unpack",
    )(first, second)


EPS = 1e-05


def turn(value):
    return value.astype(F32).T


def rms_rows(x):
    return lax.rsqrt(jnp.mean(x * x, axis=0, keepdims=True) + EPS)


def norm_back_rows(grad, x, inverse, gain):
    gain_grad = jnp.sum(grad * x * inverse, axis=1, keepdims=True)
    scaled = grad * gain
    mean = jnp.mean(scaled * x, axis=0, keepdims=True)
    return inverse * scaled - x * (inverse * inverse * inverse) * mean, gain_grad


def rotate(rows, cosine, sine):
    a, b = rows[:32], rows[32:]
    return jnp.concatenate([a * cosine - b * sine, b * cosine + a * sine], axis=0)


def head_rows(i):
    return slice(64 * i, 64 * i + 64)


def token_lanes(j):
    return slice(128 * j, 128 * j + 128)


def project_kernel(x_ref, w_ref, gain_ref, cos_ref, sin_ref, qt_ref, kv_ref, h_ref, inv_ref, raw):
    x = x_ref[...].astype(F32)
    inverse = rms_rows(x)
    inv_ref[...] = inverse
    normed = x * inverse * gain_ref[:, 0:1].astype(F32)
    h_ref[...] = normed.astype(BF16)
    rows = turn(normed).astype(BF16)
    for first, count in ((0, 512), (512, 512), (1024, 576)):
        lanes = slice(first, first + count)
        part = jnp.dot(rows, w_ref[:, lanes], preferred_element_type=F32)
        raw[lanes] = part.T
    cosine, sine = cos_ref[...], sin_ref[...]
    for g in range(KEY_VALUE_HEADS):
        for j in range(QUERY_PER_KV):
            q = rotate(raw[head_rows(3 * g + j)], cosine, sine).astype(BF16)
            qt_ref[g, 0:64, token_lanes(j)] = q * BF16(0.125)
        qt_ref[g, 64:128, :] = jnp.zeros((64, ROWS3), BF16)
        k = rotate(raw[head_rows(15 + g)], cosine, sine)
        pair = jnp.concatenate([k, raw[head_rows(20 + g)]], axis=0)
        kv_ref[g] = pair.T.astype(BF16)


def plain_params():
    return pltpu.CompilerParams(vmem_limit_bytes=VMEM_LIMIT)


def project_call(*args):
    shape = jax.ShapeDtypeStruct
    return pl.pallas_call(
        project_kernel,
        out_shape=(
            shape((5, 128, ROWS3), BF16),
            shape((5, 128, 128), BF16),
            shape((960, 128), BF16),
            shape((1, 128), F32),
        ),
        in_specs=[INV] * 5,
        out_specs=[INV] * 4,
        scratch_shapes=[pltpu.VMEM((1600, 128), F32)],
        compiler_params=plain_params(),
        name="project",
    )(*args)


def middle_kernel(
    x_ref, dy_ref, gain_ref, u_ref, l_ref, qt_ref, wo_hbm, wg_hbm, wu_hbm, wd_hbm,
    out_ref, h_ref, dg_ref, dp_ref, z_ref, dx_ref, a_ref, w_ref, delta_ref, ggain_ref,
    wo, wg, wu, wd, attended, sems,
):
    loads = []
    for i, (src, dst) in enumerate(((wo_hbm, wo), (wg_hbm, wg), (wu_hbm, wu), (wd_hbm, wd))):
        cp = pltpu.make_async_copy(src, dst, sems.at[i])
        cp.start()
        loads.append(cp)
    for g in range(KEY_VALUE_HEADS):
        for j in range(QUERY_PER_KV):
            lanes = token_lanes(j)
            attended[head_rows(3 * g + j)] = u_ref[g, 64:128, lanes] / l_ref[g, :, lanes]
    a_ref[...] = attended[...].astype(BF16)
    a_rows = attended[...].T.astype(BF16)
    dy_turned = dy_ref[...].astype(F32)
    dy_rows = dy_turned.T.astype(BF16)
    loads[0].wait()
    branch = jnp.dot(a_rows, wo[...], preferred_element_type=F32)
    x2 = x_ref[...].astype(F32) + branch.T
    inverse = rms_rows(x2)
    gain = gain_ref[:, 64:65].astype(F32)
    normed = x2 * inverse * gain
    h_ref[...] = normed.astype(BF16)
    h_rows = normed.T.astype(BF16)
    for cp in loads[1:]:
        cp.wait()

    def hidden(i, carry):
        lanes = pl.ds(pl.multiple_of(i * 512, 128), 512)
        gate = jnp.dot(h_rows, wg[:, lanes], preferred_element_type=F32)
        upper = jnp.dot(h_rows, wu[:, lanes], preferred_element_type=F32)
        dz = jnp.dot(dy_rows, wd[:, lanes], preferred_element_type=F32)
        sigma = jax.nn.sigmoid(gate)
        silu = gate * sigma
        z_ref[:, lanes] = (silu * upper).astype(BF16)
        dg_ref[:, lanes] = (dz * upper * sigma * (1.0 + gate * (1.0 - sigma))).astype(BF16)
        dp_ref[:, lanes] = (dz * silu).astype(BF16)
        return carry

    lax.fori_loop(0, 5, hidden, 0)

    def back(i, carry):
        out, grad = carry
        lanes = pl.ds(pl.multiple_of(i * 512, 128), 512)
        out = out + over_lanes(wd[:, lanes], z_ref[:, lanes])
        grad = grad + over_lanes(wg[:, lanes], dg_ref[:, lanes])
        grad = grad + over_lanes(wu[:, lanes], dp_ref[:, lanes])
        return out, grad

    out, grad = lax.fori_loop(0, 5, back, (x2, jnp.zeros((960, 128), F32)))
    out_ref[...] = out.astype(BF16)
    change, ggain_ref[...] = norm_back_rows(grad, x2, inverse, gain)
    dx = dy_turned + change
    dx_ref[...] = dx
    da = jnp.dot(wo[...], dx.astype(BF16), preferred_element_type=F32)
    for g in range(KEY_VALUE_HEADS):
        w_ref[g, :, 0:ROWS3] = qt_ref[g]
        w_ref[g, 0:64, ROWS3:] = jnp.zeros((64, ROWS3), BF16)
        for j in range(QUERY_PER_KV):
            lanes = token_lanes(j)
            rows = head_rows(3 * g + j)
            total = l_ref[g, :, lanes]
            w_ref[g, 64:128, ROWS3 + 128 * j:ROWS3 + 128 * j + 128] = (
                da[rows] / total
            ).astype(BF16)
            delta_ref[g, :, lanes] = (
                jnp.sum(da[rows] * attended[rows], axis=0, keepdims=True) / total
            )


def middle_call(*args):
    shape = jax.ShapeDtypeStruct
    return pl.pallas_call(
        middle_kernel,
        out_shape=(
            shape((960, 128), BF16),
            shape((960, 128), BF16),
            shape((128, 2560), BF16),
            shape((128, 2560), BF16),
            shape((128, 2560), BF16),
            shape((960, 128), F32),
            shape((960, 128), BF16),
            shape((5, 128, 2 * ROWS3), BF16),
            shape((5, 1, ROWS3), F32),
            shape((960, 1), F32),
        ),
        in_specs=[INV] * 6 + [ANY] * 4,
        out_specs=[INV] * 10,
        scratch_shapes=[
            pltpu.VMEM((960, 960), BF16),
            pltpu.VMEM((960, 2560), BF16),
            pltpu.VMEM((960, 2560), BF16),
            pltpu.VMEM((960, 2560), BF16),
            pltpu.VMEM((960, 128), F32),
            dma_sems(4),
        ],
        compiler_params=plain_params(),
        name="middle",
    )(*args)


def finish_kernel(
    dq_ref, pair_ref, cos_ref, sin_ref, w_ref, x_ref, inv_ref, gain_ref, h_ref, dx_ref, a_ref,
    out_ref, lhs_ref, rhs_ref, ggain_ref,
):
    cosine, sine = cos_ref[...], -sin_ref[...]
    rhs_ref[0:1600, 128:256] = jnp.zeros((1600, 128), BF16)
    rhs_ref[1600:2560, 0:128] = jnp.zeros((960, 128), BF16)
    dx = dx_ref[...]
    rhs_ref[1600:2560, 128:256] = dx.astype(BF16)
    lhs_ref[:, 0:128] = h_ref[...]
    lhs_ref[:, 128:256] = a_ref[...]
    for g in range(KEY_VALUE_HEADS):
        for j in range(QUERY_PER_KV):
            rows = rotate(dq_ref[g, 0:64, token_lanes(j)] * 0.125, cosine, sine)
            rhs_ref[head_rows(3 * g + j), 0:128] = rows.astype(BF16)
        pair = turn(pair_ref[g])
        rhs_ref[head_rows(15 + g), 0:128] = rotate(pair[:64], cosine, sine).astype(BF16)
        rhs_ref[head_rows(20 + g), 0:128] = pair[64:].astype(BF16)
    grad = jnp.dot(w_ref[...], rhs_ref[0:1600, 0:128], preferred_element_type=F32)
    change, ggain_ref[...] = norm_back_rows(
        grad, x_ref[...].astype(F32), inv_ref[...], gain_ref[:, 0:1].astype(F32)
    )
    out_ref[...] = (dx + change).astype(BF16)


def finish_call(*args):
    shape = jax.ShapeDtypeStruct
    return pl.pallas_call(
        finish_kernel,
        out_shape=(
            shape((960, 128), BF16),
            shape((960, 256), BF16),
            shape((2560, 256), BF16),
            shape((960, 1), F32),
        ),
        in_specs=[INV] * 11,
        out_specs=[INV] * 4,
        compiler_params=plain_params(),
        name="finish",
    )(*args)


def shards(
    tokens, positions, w_query, key_weight, value_weight, w_output, gain_attn,
    w_gate, w_up, w_down, gain_mlp, cotangent,
):
    owned_positions = positions[0]
    w_one = jnp.concatenate([w_query, key_weight, value_weight], axis=1)
    gains = jnp.concatenate(
        [
            jnp.broadcast_to(gain_attn[:, None], (240, 64)),
            jnp.broadcast_to(gain_mlp[:, None], (240, 64)),
        ],
        axis=1,
    )
    w_qkv, gains = first_call(w_one, gains)
    half_size = HEAD_SIZE // 2
    frequency = 100000.0 ** (-(jnp.arange(half_size, dtype=F32) * 2.0 / HEAD_SIZE))
    angles = frequency[:, None] * owned_positions.astype(F32)[None, :]
    cosine, sine = jnp.cos(angles), jnp.sin(angles)
    x_turned = tokens[0].T
    dy_turned = cotangent[0].T

    qt, kv_own, h_one, inverse_one = project_call(x_turned, w_qkv, gains, cosine, sine)
    kv_all, bias, u_all, top, total, wo_all, wg_all, wu_all, wd_turned = forward_call(
        kv_own, qt, jnp.broadcast_to(owned_positions[None], (8, 128)),
        w_output, w_gate, w_up, w_down.T,
    )
    out, h_two, dg, dp, z, dx, a, w_back, delta, gain_two = middle_call(
        x_turned, dy_turned, gains, u_all, total, qt, wo_all, wg_all, wu_all, wd_turned
    )
    dq, own_pairs, mlp_own = backward_call(
        kv_all, w_back, bias, top, delta, h_two, dg, dp, dy_turned, z
    )
    grad_in, lhs, rhs, gain_one = finish_call(
        dq, own_pairs, cosine, sine, w_qkv, x_turned, inverse_one, gains, h_one, dx, a
    )
    term_gains = jnp.concatenate([gain_one, gain_two], axis=1).astype(BF16)
    gain_rows = jnp.pad(
        term_gains.reshape(4, 240, 2).transpose(0, 2, 1), ((0, 0), (0, 14), (0, 16))
    ).reshape(64, 256)
    packed = last_call(lhs, rhs, gain_rows, mlp_own)
    (
        sum_query, sum_key, sum_value, sum_output, sum_gains, sum_gate, sum_up, sum_down
    ) = unpack_call(*packed)
    return (
        out.T[None], grad_in.T[None], sum_query, sum_key, sum_value, sum_output,
        sum_gains[0, :240], sum_gate, sum_up, sum_down.T, sum_gains[1, :240],
    )


def solution(mesh):
    in_specs = (
        P("dp", "ctx", None), P("dp", "ctx"),
        P("dp", None), P("dp", None), P("dp", None), P("dp", None), P("dp"),
        P("dp", None), P("dp", None), P("dp", None), P("dp"),
        P("dp", "ctx", None),
    )
    out_specs = (
        P("dp", "ctx", None), P("dp", "ctx", None),
        P("dp", None), P("dp", None), P("dp", None), P("dp", None), P("dp"),
        P("dp", None), P("dp", None), P("dp", None), P("dp"),
    )
    return jax.shard_map(shards, mesh=mesh, in_specs=in_specs, out_specs=out_specs, check_vma=False)
```

time: 368 us -> 319 us (0.87); the launches traced: 361 us -> 318 us
  matrix products: 39.1 us -> 0 us
  Pallas kernels: 263 us -> 301 us
  local copies, waits for them, and re-layouts: 37.6 us -> 12.7 us
  other arithmetic: 19.9 us -> 3.6 us
    dot_general x15 -> x0, matrix products: 39.1 us -> none  [matrix_product(): return jnp.dot(left, right, preferred_element_type=F32)]
    pallas_call x1 -> x4, Pallas kernels: 7.21 us -> 34.6 us  [the longest x1 17.9 us: middle_call(): pl.pallas_call(middle_kernel, out_shape=(shape((960, 128), BF16), shape((...]
    pallas_call x1, Pallas kernels: 91.3 us -> 103 us  [backward_call(): pl.pallas_call(backward_kernel, out_shape=(shape((5, 128, ROWS3), F32), s...]
    convert_element_type x2 -> x0, local copies, waits for them, and re-layouts: 8.09 us -> none  [the longest x1 7.88 us: shards(): term_down = matrix_product(hidden.T, grad_low).astype(BF16)]
    pallas_call x1, Pallas kernels: 24.5 us -> 17.8 us  [first_call(): pl.pallas_call(first_kernel, out_shape=(jax.ShapeDtypeStruct((960, 1600),...]
    slice x10 -> x1, local copies, waits for them, and re-layouts: 7.81 us -> 1.34 us  [shards(): sum_gains[1, :240]]
    unnamed x57 -> x7, local copies, waits for them, and re-layouts: 10.6 us -> 5.88 us
    pallas_call x1, Pallas kernels: 70.3 us -> 74.1 us  [forward_call(): pl.pallas_call(forward_kernel, out_shape=(shape((2, 4, 4, 5, 128, 128), B...]
where the time goes in v1:
time: 319 us; the launch traced here: 318 us
  Pallas kernels  301 us (94%)
  local copies, waits for them, and re-layouts  12.7 us (4%)
  other arithmetic  3.6 us (1%)
    pallas_call x1, Pallas kernels, backward_call(): pl.pallas_call(backward_kernel, out_shape=(shape((5, 128, ROWS3), F32), s...  103 us
    pallas_call x1, Pallas kernels, forward_call(): pl.pallas_call(forward_kernel, out_shape=(shape((2, 4, 4, 5, 128, 128), B...  74.1 us
    pallas_call x1, Pallas kernels, last_call(): pl.pallas_call(last_kernel, out_shape=(shape((2, 4, 4, 5, 1, 32, 128), BF...  71.9 us
    pallas_call x1, Pallas kernels, middle_call(): pl.pallas_call(middle_kernel, out_shape=(shape((960, 128), BF16), shape((...  17.9 us
    pallas_call x1, Pallas kernels, first_call(): pl.pallas_call(first_kernel, out_shape=(jax.ShapeDtypeStruct((960, 1600),...  17.8 us
    pallas_call x1, Pallas kernels, unpack_call(): pl.pallas_call(unpack_kernel, out_shape=tuple((jax.ShapeDtypeStruct(s, F3...  7.22 us

profile of v1, /device:TPU:0, one launch (start us, length us, event | category | flops | bytes accessed | tf_op | source)
XLA Modules:
  0.0 318.2 jit_solution(10531617856366936104)
XLA Ops:
  0.6 0.7 convert_bitcast_fusion
  1.3 1.3 broadcast_in_dim.30.pos_ref
  2.6 0.7 multiply_sine_fusion
  3.3 0.7 broadcast_in_dim.12
  4.1 0.8 broadcast_in_dim.13
  4.8 0.7 pad_maximum_fusion.gain_ref
  5.5 1.1 copy.29
  6.6 1.1 copy.30
  7.7 2.0 concatenate.15.w_ref
  9.6 17.8 %gather_first.1 = (bf16[960,1600]{1,0:T(8,128)(2,1)}, bf16[960,128]{1,0:T(8,128)(2,1)}) custom-call(bf16[240,1600]{1,0:T(8,128)(2,1)} %concatenate.15.w_ref, bf16[240,128]{1,0:T(8,128)(2,1)} %pad_maximum_fusion.gain_ref), custom_call_target="tpu_custom_call" | custom-call | tf_op jit(solution)/shard_map/gather_first/pallas_call | solution.py:466
  27.4 3.9 %project.1 = (bf16[5,128,384]{2,1,0:T(8,128)(2,1)}, bf16[5,128,128]{2,1,0:T(8,128)(2,1)}, bf16[960,128]{1,0:T(8,128)(2,1)}, f32[1,128]{1,0:T(1,128)}) custom-call(bf16[960,128]{1,0:T(8,128)(2,1)} %bitcast.22, bf16[960,1600]{1,0:T(8,128)(2,1)} %get-tuple-element.54.w_ref, bf16[960,128]{1,0:T(8,128)(2,1)} %get-tuple-element.53.gain_ref, ...), custom_call_target="tpu_custom_call" | custom-call | tf_op jit(solution)/shard_map/project/pallas_call | solution.py:1121
  31.3 74.1 %attention_forward.1 = (bf16[2,4,4,5,128,128]{5,4,3,2,1,0:T(8,128)(2,1)}, f32[4096,128]{1,0:T(8,128)}, f32[5,128,384]{2,1,0:T(8,128)}, f32[5,1,384]{2,1,0:T(1,12...) custom-call(bf16[5,128,128]{2,1,0:T(8,128)(2,1)} %get-tuple-element., ...), custom_call_target="tpu_custom_call" | custom-call | tf_op jit(solution)/shard_map/attention_forward/pallas_call | solution.py:578
  105.4 17.9 %middle.1 = (bf16[960,128]{1,0:T(8,128)(2,1)}, bf16[960,128]{1,0:T(8,128)(2,1)}, bf16[128,2560]{1,0:T(8,128)(2,1)}, bf16[128,2560]{1,0:T(8,128)(2,1)}, bf16[128,...) custom-call(bf16[960,128]{1,0:T(8,128)(2,1)} %bitcast.23, ...), custom_call_target="tpu_custom_call" | custom-call | tf_op jit(solution)/shard_map/middle/pallas_call | solution.py:1211
  123.3 102.8 %attention_backward.1 = (f32[5,128,384]{2,1,0:T(8,128)}, bf16[5,128,128]{2,1,0:T(8,128)(2,1)}, bf16[5,3,32,128]{3,2,1,0:T(8,128)(2,1)}) custom-call(bf16[2,4,4,5,128,128]{5,4,3,2,1,0:T(8,128)(2,1)} %get-tuple-element.64.kv_ref, bf16[5,128,768]{2,1,0:T(8,128)(2,1)} %get-tuple-element.65.w_ref, f32[4096,128]{1,0:T(8,128)} %get-tuple-element.66.bias_ref, ...), custom_call_target="tpu_custom_call" | custom-call | tf_op jit(solution)/shard_map/attention_backward/pallas_call | solution.py:936
  226.1 0.0 copy-start
  226.1 5.6 %finish.1 = (bf16[960,128]{1,0:T(8,128)(2,1)}, bf16[960,256]{1,0:T(8,128)(2,1)}, bf16[2560,256]{1,0:T(8,128)(2,1)}, f32[960,1]{1,0:T(8,128)}) custom-call(f32[5,128,384]{2,1,0:T(8,128)} %get-tuple-element.73.dq_ref, bf16[5,128,128]{2,1,0:T(8,128)(2,1)} %get-tuple-element.74.pair_ref, f32[32,128]{1,0:T(8,128)} %get-tuple-element.120.cos_ref, ...), custom_call_target="tpu_custom_call" | custom-call | tf_op jit(solution)/shard_map/finish/pallas_call | solution.py:1267
  231.7 1.2 convert_reduce_fusion.1
  233.0 0.1 concatenate.17
  233.0 0.0 copy-done
  233.1 0.2 convert_reduce_fusion
  233.3 0.1 concatenate.18
  233.4 0.6 pad.4.clone
  234.0 71.9 %last_gradients.1 = (bf16[2,4,4,5,1,32,128]{6,5,4,3,2,1,0:T(8,128)(2,1)}, bf16[2,4,4,5,3,32,128]{6,5,4,3,2,1,0:T(8,128)(2,1)}) custom-call(bf16[960,256]{1,0:T(8,128)(2,1)} %get-tuple-element.80.lhs_ref, bf16[2560,256]{1,0:T(8,128)(2,1)} %get-tuple-element.81.rhs_ref, bf16[64,256]{1,0:T(8,128)(2,1)} %bitcast.28, ...), custom_call_target="tpu_custom_call" | custom-call | tf_op jit(solution)/shard_map/last_gradients/pallas_call | solution.py:1004
  305.9 7.2 %unpack.1 = (f32[240,960]{1,0:T(8,128)}, f32[240,320]{1,0:T(8,128)}, f32[240,320]{1,0:T(8,128)}, f32[240,960]{1,0:T(8,128)}, f32[16,256]{1,0:T(8,128)}, /*index=...) custom-call(bf16[2,4,4,5,1,32,128]{6,5,4,3,2,1,0:T(8,128)(2,1)} %get-tuple-element.85.first, ...), custom_call_target="tpu_custom_call" | custom-call | tf_op jit(solution)/shard_map/unpack/pallas_call | solution.py:1052
  313.1 1.3 fusion
  314.5 1.9 copy.32
  316.3 1.9 copy.33
  (3 shorter events, 0.0 us)
Async XLA Ops:
  226.1 6.9 %copy-start = (f32[960,1]{1,0:T(8,128)S(1)}, f32[960,1]{1,0:T(8,128)}, u32[]{:S(2)}) copy-start(f32[960,1]{1,0:T(8,128)} %get-tuple-element.83) | copy-start | bytes 11524

commit v2 on v1

--- a/solution.py
+++ b/solution.py
@@ -172,7 +172,7 @@
             iy, ix = i // xn, i % xn
             here = (by.start + iy, bx.start + ix, bz) + tail
             there = head + (py.start + iy, px.start + ix, pz)
-            acc[here] = (acc[here].astype(F32) + buf[there].astype(F32)).astype(BF16)
+            acc[here] = acc[here] + buf[there]
             return carry
 
         if yn * xn == 1:
@@ -314,7 +314,7 @@
         self.flying = {}
         self.sent = []
 
-    def start(self, part, stage):
+    def start(self, part, stage, pick=slice(None)):
         dims = order(self.ydim, part)
         state = SINGLE
         for d in dims[:stage]:
@@ -322,9 +322,9 @@
         to = partner(self.co, dims[stage])
         out = []
         for box, _, _ in boxes(state, self.co, "yh"):
-            ref = self.buf.at[box + (part,)]
+            ref = self.buf.at[box + (part, pick)]
             out.append(self.sems.copy(ref, ref, to))
-        self.flying[part, stage] = out
+        self.flying.setdefault((part, stage), []).extend(out)
         self.sent += out
 
     def finish(self, part, stage):
@@ -408,7 +408,12 @@
                     src.at[pl.ds(h, n - h)], self.block(i, me, h, n - h), partner(co, "y3")
                 )
             self.stage.append((one, two))
-            whole = self.block(i, me, 0, n)
+
+    def share_own(self):
+        co = self.co
+        me = co["yl"] * 2 + co["c"]
+        for i, (src, dst, h, lanes) in enumerate(self.items):
+            whole = self.block(i, me, 0, src.shape[0])
             self.waits.append(self.sems.copy(src, whole, partner(co, "core")))
             cp = pltpu.make_async_copy(src, whole, self.local.at[i])
             cp.start()
@@ -435,6 +440,76 @@
             cp.wait()
 
 
+class Spread:
+    CUTS = ((0, 128), (128, 112))
+
+    def __init__(self, src, dst, lanes, axis, sems, local, co):
+        self.src, self.dst, self.lanes, self.axis = src, dst, lanes, axis
+        self.sems, self.local, self.co = sems, local, co
+        self.waits = []
+
+    def piece(self, q, t, first, count):
+        rows = (t if self.lanes else q) * 240 + first
+        lanes = (q if self.lanes else t) * 640
+        return self.dst.at[
+            pl.ds(pl.multiple_of(rows, 16), count), pl.ds(pl.multiple_of(lanes, 128), 640)
+        ]
+
+    def own(self, t, first, count):
+        if self.lanes:
+            return self.src.at[pl.ds(pl.multiple_of(240 * t + first, 16), count)]
+        return self.src.at[pl.ds(first, count), pl.ds(pl.multiple_of(640 * t, 128), 640)]
+
+    def block(self, q):
+        if self.lanes:
+            return self.dst.at[:, pl.ds(pl.multiple_of(640 * q, 128), 640)]
+        return self.dst.at[pl.ds(pl.multiple_of(240 * q, 16), 240)]
+
+    def start(self):
+        co = self.co
+        me, t = co["yl"] * 2 + co["c"], co[self.axis]
+        self.flying = [
+            self.sems.copy(self.own(t, *cut), self.piece(me, t, *cut), partner(co, way))
+            for way, cut in zip(("y1", "y3"), self.CUTS)
+        ]
+        self.sent = list(self.flying)
+
+    def share_own(self):
+        co = self.co
+        whole = self.block(co["yl"] * 2 + co["c"])
+        self.waits.append(self.sems.copy(self.src, whole, partner(co, "core")))
+        cp = pltpu.make_async_copy(self.src, whole, self.local)
+        cp.start()
+        self.waits.append(cp)
+
+    def share(self, step):
+        co = self.co
+        t = co[self.axis]
+        q = (1 - co["yl"]) * 2 + co["c"]
+        for cp in self.flying:
+            cp.wait_recv()
+        self.flying = []
+        for cut, edges, other in zip(self.CUTS, ("13", "31"), (flip(t), 3 - t)):
+            to = partner(co, self.axis + edges[step])
+            for at in (t, other)[:step + 1]:
+                ref = self.piece(q, at, *cut)
+                self.flying.append(self.sems.copy(ref, ref, to))
+        self.sent += self.flying
+
+    def forward(self):
+        co = self.co
+        for cp in self.flying:
+            cp.wait_recv()
+        ref = self.block((1 - co["yl"]) * 2 + co["c"])
+        self.waits.append(self.sems.copy(ref, ref, partner(co, "core")))
+
+    def finish(self):
+        for cp in self.sent:
+            cp.wait_send()
+        for cp in self.waits:
+            cp.wait()
+
+
 def params(cid):
     return pltpu.CompilerParams(
         collective_id=cid, has_side_effects=True, vmem_limit_bytes=VMEM_LIMIT
@@ -456,6 +531,7 @@
         [(gain_ref, gain_out, 240, False), (w_ref, w_out, 128, False)],
         Sems(send, recv), local, co,
     )
+    gather.share_own()
     gather.start()
     gather.forward(0)
     gather.forward(1)
@@ -499,24 +575,34 @@
 ):
     co = coords()
     greet(co, ("x1", "x3", "z1", "z3", "y2", "core", "y1", "y3"))
+    wsems = Sems(wsend, wrecv)
     weights = Gather(
         [
             (wo_ref, wo_all, 128, False),
             (wg_ref, wg_all, 128, False),
-            (wu_ref, wu_all, 128, False),
-            (wd_ref, wd_all, 480, True),
         ],
-        Sems(wsend, wrecv), local, co,
+        wsems, local, co,
+    )
+    spreads = (
+        Spread(wu_ref, wu_all, False, "x", wsems, local.at[2], co),
+        Spread(wd_ref, wd_all, True, "z", wsems, local.at[3], co),
     )
     here = (co["yh"], co["x"], co["z"])
     kv_all[here] = kv_ref[...]
     places[here] = pos_ref[...]
     ag = PlaneGather(kv_all, places, Sems(send, recv), co)
+    for item in (weights,) + spreads:
+        item.share_own()
     ag.first()
     for part in range(4):
         ag.start(part, 0)
+    for spread in spreads:
+        spread.start()
     weights.start()
     for stage in range(1, 4):
+        if stage == 3:
+            for spread in spreads:
+                spread.share(0)
         for part in range(4):
             ag.finish(part, stage - 1)
             ag.start(part, stage)
@@ -540,6 +626,9 @@
         if g > 0:
             for part in range(4):
                 ag.finish(part, 3, g)
+        if g == 1:
+            for spread in spreads:
+                spread.share(1)
         if g == 4:
             weights.forward(0)
             weights.forward(1)
@@ -552,7 +641,9 @@
             scores[pl.ds(i * CHUNK, CHUNK)] = s
             return jnp.maximum(top, jnp.max(s.reshape(CHUNK // 8, 8, ROWS3), axis=0))
 
-        top = lax.fori_loop(0, 8, score, jnp.full((8, ROWS3), -1e30, F32))
+        top = lax.fori_loop(
+            0, 8, score, jnp.full((8, ROWS3), -1e30, F32), unroll=8
+        )
         top = jnp.max(top, axis=0, keepdims=True)
 
         def weigh(i, carry):
@@ -563,14 +654,16 @@
             return total, u + over_dim0(kv, e.astype(BF16))
 
         carry = (jnp.zeros((8, ROWS3), F32), jnp.zeros((128, ROWS3), F32))
-        total, u = lax.fori_loop(0, 8, weigh, carry)
+        total, u = lax.fori_loop(0, 8, weigh, carry, unroll=8)
         u_ref[g] = u
         m_ref[g] = top
         l_ref[g] = jnp.sum(total, axis=0, keepdims=True)
-    weights.forward(2)
-    weights.forward(3)
+    for spread in spreads:
+        spread.forward()
     ag.drain()
     weights.finish()
+    for spread in spreads:
+        spread.finish()
 
 
 def forward_call(kv, qt, pos, wo, wg, wu, wd):
@@ -593,7 +686,7 @@
         scratch_shapes=[
             pltpu.VMEM((4096, ROWS3), F32),
             pltpu.VMEM((2, 4, 4, 8, 128), jnp.int32),
-            dma_sems(128), dma_sems(128), dma_sems(20), dma_sems(20), dma_sems(4),
+            dma_sems(128), dma_sems(128), dma_sems(32), dma_sems(32), dma_sems(4),
         ],
         compiler_params=params(2),
         name="attention_forward",
@@ -650,7 +743,7 @@
             out[yl, pl.ds(0, value.shape[0]), part_lanes(kind, p)] = value
             return carry
 
-        lax.fori_loop(0, 5, step, 0)
+        lax.fori_loop(0, 5, step, 0, unroll=5)
         if kind == GAIN:
             out[yl, 240:256, :] = jnp.zeros((16, 2560), BF16)
             rows = pl.ds(pl.multiple_of(16 * q, 16), 16)
@@ -683,7 +776,7 @@
                     put(yl, x, z, p, block)
             return carry
 
-        lax.fori_loop(0, 5, step, 0)
+        lax.fori_loop(0, 5, step, 0, unroll=5)
 
 
 class GradSum:
@@ -813,9 +906,7 @@
             cp.wait_recv()
 
         def add(here, there):
-            self.acc[(yl,) + here] = (
-                self.acc[(yl,) + here].astype(F32) + self.ybuf[there].astype(F32)
-            ).astype(BF16)
+            self.acc[(yl,) + here] = self.acc[(yl,) + here] + self.ybuf[there]
 
         if self.late:
             add((co["x"], co["z"]), (slice(None),))
@@ -887,7 +978,7 @@
     slabs[0].fold()
     slabs[1].fold()
     pairs = PairSum(acc, own_ref, last, bufs, Sems(send, recv), co)
-    starts = (2, 3, 5)
+    starts = (2, 4, 8)
     for g in range(KEY_VALUE_HEADS):
         w = w_ref[g]
         top, delta = m_ref[g], delta_ref[g]
@@ -906,7 +997,7 @@
 
         dq = jnp.zeros((128, ROWS3), F32)
         for half in range(2):
-            dq = lax.fori_loop(4 * half, 4 * half + 4, step, dq)
+            dq = lax.fori_loop(4 * half, 4 * half + 4, step, dq, unroll=4)
             if half == 1:
                 dq_ref[g] = dq
                 pairs.advance(g)
@@ -963,7 +1054,6 @@
     greet(co, GRAD_DIMS)
     here = (co["yh"], co["x"], co["z"])
     grad = GradSum(LAST, ((lhs_ref, rhs_ref),), gain_ref, rest[4:], co)
-    grad.begin(0)
     mlp_out[here] = mlp_ref[...]
     mlp = AllGather(mlp_out, Sems(msend, mrecv), co)
     for part in range(5):
@@ -972,16 +1062,25 @@
     def mlp_stage(stage):
         for part in range(5):
             mlp.finish(part, stage)
-            if stage < 4:
+            if stage < 3:
                 mlp.start(part, stage + 1)
 
+    def mlp_last(slab):
+        for part in range(5):
+            mlp.start(part, 4, slab)
+
+    grad.begin(0)
+    mlp_stage(0)
+    mlp_stage(1)
     grad.fold(0)
     grad.launch()
-    mlp_stage(0)
-    for stage in range(5):
-        grad.stage(stage)
-        if stage < 4:
-            mlp_stage(stage + 1)
+    mlp_stage(2)
+    grad.stage(0)
+    grad.stage(1)
+    mlp_stage(3)
+    for i in range(3):
+        mlp_last(i)
+        grad.stage(2 + i)
     grad.halve()
     grad.half.wait_recv()
     for p in range(5):
@@ -994,6 +1093,7 @@
             ag.finish(part, stage)
             if stage < 4:
                 ag.start(part, stage + 1)
+    mlp_stage(4)
     grad.drain()
     mlp.drain()
     ag.drain()
@@ -1009,7 +1109,7 @@
         ),
         in_specs=[INV] * 4,
         out_specs=[INV, INV],
-        scratch_shapes=[dma_sems(48)] * 4 + grad_scratch(LAST),
+        scratch_shapes=[dma_sems(64)] * 4 + grad_scratch(LAST),
         compiler_params=params(4),
         name="last_gradients",
     )(*args)
@@ -1175,7 +1275,7 @@
         dp_ref[:, lanes] = (dz * silu).astype(BF16)
         return carry
 
-    lax.fori_loop(0, 5, hidden, 0)
+    lax.fori_loop(0, 5, hidden, 0, unroll=5)
 
     def back(i, carry):
         out, grad = carry
@@ -1185,7 +1285,9 @@
         grad = grad + over_lanes(wu[:, lanes], dp_ref[:, lanes])
         return out, grad
 
-    out, grad = lax.fori_loop(0, 5, back, (x2, jnp.zeros((960, 128), F32)))
+    out, grad = lax.fori_loop(
+        0, 5, back, (x2, jnp.zeros((960, 128), F32)), unroll=5
+    )
     out_ref[...] = out.astype(BF16)
     change, ggain_ref[...] = norm_back_rows(grad, x2, inverse, gain)
     dx = dy_turned + change

time: 319 us -> 303 us (0.950)
  Pallas kernels: 301 us -> 283 us
    pallas_call x1, Pallas kernels: 103 us -> 92 us  [backward_call(): pl.pallas_call(backward_kernel, out_shape=(shape((5, 128, ROWS3), F32), s...]
    pallas_call x1, Pallas kernels: 74.1 us -> 69 us  [forward_call(): pl.pallas_call(forward_kernel, out_shape=(shape((2, 4, 4, 5, 128, 128), B...]
where the time goes in v2:
time: 303 us; the launch traced here: 300 us
  Pallas kernels  283 us (93%)
  local copies, waits for them, and re-layouts  12.7 us (4%)
  other arithmetic  3.6 us (1%)
    pallas_call x1, Pallas kernels, backward_call(): pl.pallas_call(backward_kernel, out_shape=(shape((5, 128, ROWS3), F32), s...  92 us
    pallas_call x1, Pallas kernels, last_call(): pl.pallas_call(last_kernel, out_shape=(shape((2, 4, 4, 5, 1, 32, 128), BF...  70.9 us
    pallas_call x1, Pallas kernels, forward_call(): pl.pallas_call(forward_kernel, out_shape=(shape((2, 4, 4, 5, 128, 128), B...  69 us
    pallas_call x1, Pallas kernels, first_call(): pl.pallas_call(first_kernel, out_shape=(jax.ShapeDtypeStruct((960, 1600),...  17.8 us
    pallas_call x1, Pallas kernels, middle_call(): pl.pallas_call(middle_kernel, out_shape=(shape((960, 128), BF16), shape((...  16.3 us
    pallas_call x1, Pallas kernels, unpack_call(): pl.pallas_call(unpack_kernel, out_shape=tuple((jax.ShapeDtypeStruct(s, F3...  7.22 us

profile of v2, /device:TPU:0, one launch (start us, length us, event | category | flops | bytes accessed | tf_op | source)
XLA Modules:
  0.0 299.9 jit_solution(2880560504389313740)
XLA Ops:
  0.6 0.7 convert_bitcast_fusion
  1.3 1.3 broadcast_in_dim.30.pos_ref
  2.6 0.7 multiply_sine_fusion
  3.3 0.7 broadcast_in_dim.12
  4.1 0.8 broadcast_in_dim.13
  4.8 0.7 pad_maximum_fusion.gain_ref
  5.5 1.1 copy.29
  6.6 1.1 copy.30
  7.7 2.0 concatenate.15.w_ref
  9.6 17.8 %gather_first.1 = (bf16[960,1600]{1,0:T(8,128)(2,1)}, bf16[960,128]{1,0:T(8,128)(2,1)}) custom-call(bf16[240,1600]{1,0:T(8,128)(2,1)} %concatenate.15.w_ref, bf16[240,128]{1,0:T(8,128)(2,1)} %pad_maximum_fusion.gain_ref), custom_call_target="tpu_custom_call" | custom-call | tf_op jit(solution)/shard_map/gather_first/pallas_call | solution.py:542
  27.4 3.9 %project.1 = (bf16[5,128,384]{2,1,0:T(8,128)(2,1)}, bf16[5,128,128]{2,1,0:T(8,128)(2,1)}, bf16[960,128]{1,0:T(8,128)(2,1)}, f32[1,128]{1,0:T(1,128)}) custom-call(bf16[960,128]{1,0:T(8,128)(2,1)} %bitcast.22, bf16[960,1600]{1,0:T(8,128)(2,1)} %get-tuple-element.54.w_ref, bf16[960,128]{1,0:T(8,128)(2,1)} %get-tuple-element.53.gain_ref, ...), custom_call_target="tpu_custom_call" | custom-call | tf_op jit(solution)/shard_map/project/pallas_call | solution.py:1221
  31.3 69.0 %attention_forward.1 = (bf16[2,4,4,5,128,128]{5,4,3,2,1,0:T(8,128)(2,1)}, f32[4096,128]{1,0:T(8,128)}, f32[5,128,384]{2,1,0:T(8,128)}, f32[5,1,384]{2,1,0:T(1,12...) custom-call(bf16[5,128,128]{2,1,0:T(8,128)(2,1)} %get-tuple-element., ...), custom_call_target="tpu_custom_call" | custom-call | tf_op jit(solution)/shard_map/attention_forward/pallas_call | solution.py:671
  100.3 16.3 %middle.1 = (bf16[960,128]{1,0:T(8,128)(2,1)}, bf16[960,128]{1,0:T(8,128)(2,1)}, bf16[128,2560]{1,0:T(8,128)(2,1)}, bf16[128,2560]{1,0:T(8,128)(2,1)}, bf16[128,...) custom-call(bf16[960,128]{1,0:T(8,128)(2,1)} %bitcast.23, ...), custom_call_target="tpu_custom_call" | custom-call | tf_op jit(solution)/shard_map/middle/pallas_call | solution.py:1313
  116.6 92.0 %attention_backward.1 = (f32[5,128,384]{2,1,0:T(8,128)}, bf16[5,128,128]{2,1,0:T(8,128)(2,1)}, bf16[5,3,32,128]{3,2,1,0:T(8,128)(2,1)}) custom-call(bf16[2,4,4,5,128,128]{5,4,3,2,1,0:T(8,128)(2,1)} %get-tuple-element.64.kv_ref, bf16[5,128,768]{2,1,0:T(8,128)(2,1)} %get-tuple-element.65.w_ref, f32[4096,128]{1,0:T(8,128)} %get-tuple-element.66.bias_ref, ...), custom_call_target="tpu_custom_call" | custom-call | tf_op jit(solution)/shard_map/attention_backward/pallas_call | solution.py:1027
  208.6 0.0 copy-start
  208.7 5.6 %finish.1 = (bf16[960,128]{1,0:T(8,128)(2,1)}, bf16[960,256]{1,0:T(8,128)(2,1)}, bf16[2560,256]{1,0:T(8,128)(2,1)}, f32[960,1]{1,0:T(8,128)}) custom-call(f32[5,128,384]{2,1,0:T(8,128)} %get-tuple-element.73.dq_ref, bf16[5,128,128]{2,1,0:T(8,128)(2,1)} %get-tuple-element.74.pair_ref, f32[32,128]{1,0:T(8,128)} %get-tuple-element.120.cos_ref, ...), custom_call_target="tpu_custom_call" | custom-call | tf_op jit(solution)/shard_map/finish/pallas_call | solution.py:1369
  214.2 1.2 convert_reduce_fusion.1
  215.5 0.1 concatenate.17
  215.5 0.0 copy-done
  215.6 0.2 convert_reduce_fusion
  215.8 0.1 concatenate.18
  215.9 0.6 pad.4.clone
  216.5 70.9 %last_gradients.1 = (bf16[2,4,4,5,1,32,128]{6,5,4,3,2,1,0:T(8,128)(2,1)}, bf16[2,4,4,5,3,32,128]{6,5,4,3,2,1,0:T(8,128)(2,1)}) custom-call(bf16[960,256]{1,0:T(8,128)(2,1)} %get-tuple-element.80.lhs_ref, bf16[2560,256]{1,0:T(8,128)(2,1)} %get-tuple-element.81.rhs_ref, bf16[64,256]{1,0:T(8,128)(2,1)} %bitcast.28, ...), custom_call_target="tpu_custom_call" | custom-call | tf_op jit(solution)/shard_map/last_gradients/pallas_call | solution.py:1104
  287.4 7.2 %unpack.1 = (f32[240,960]{1,0:T(8,128)}, f32[240,320]{1,0:T(8,128)}, f32[240,320]{1,0:T(8,128)}, f32[240,960]{1,0:T(8,128)}, f32[16,256]{1,0:T(8,128)}, /*index=...) custom-call(bf16[2,4,4,5,1,32,128]{6,5,4,3,2,1,0:T(8,128)(2,1)} %get-tuple-element.85.first, ...), custom_call_target="tpu_custom_call" | custom-call | tf_op jit(solution)/shard_map/unpack/pallas_call | solution.py:1152
  294.6 1.3 fusion
  296.0 1.9 copy.32
  297.8 1.9 copy.33
  (3 shorter events, 0.0 us)
Async XLA Ops:
  208.6 6.9 %copy-start = (f32[960,1]{1,0:T(8,128)S(1)}, f32[960,1]{1,0:T(8,128)}, u32[]{:S(2)}) copy-start(f32[960,1]{1,0:T(8,128)} %get-tuple-element.83) | copy-start | bytes 11524

commit v3 on v2

--- a/solution.py
+++ b/solution.py
@@ -589,7 +589,7 @@
     )
     here = (co["yh"], co["x"], co["z"])
     kv_all[here] = kv_ref[...]
-    places[here] = pos_ref[...]
+    places[here] = jnp.broadcast_to(pos_ref[...], (8, 128))
     ag = PlaneGather(kv_all, places, Sems(send, recv), co)
     for item in (weights,) + spreads:
         item.share_own()
@@ -1115,7 +1115,8 @@
     )(*args)
 
 
-def unpack_kernel(first, second, q_ref, k_ref, v_ref, o_ref, gain_ref, *outs):
+def unpack_kernel(first, second, q_ref, k_ref, v_ref, o_ref, gain_ref, *rest):
+    outs, pairs = rest[:-1], rest[-1]
     for x in range(4):
         for yh in range(2):
             at = 64 * x + 32 * yh
@@ -1123,10 +1124,13 @@
                 [first[yh, x, z, p, 0].astype(F32) for p in range(5) for z in range(4)], axis=1
             )
             rows = min(32, 240 - at)
-            for ref, lane in ((q_ref, 0), (k_ref, 960), (v_ref, 1280), (o_ref, 1600)):
+            for ref, lane in ((q_ref, 0), (o_ref, 1600)):
                 ref[at:at + rows] = value[:rows, lane:lane + ref.shape[1]]
+            pairs[at:at + 32] = value[:, 896:1664]
             if rows < 32:
                 gain_ref[...] = value[rows:, :256]
+    k_ref[...] = pairs[:, 0:384].T[64:384, :240]
+    v_ref[...] = pairs[:, 384:768].T[:320, :240]
     for i, kind in enumerate(MLP):
 
         def part(p, carry):
@@ -1147,13 +1151,14 @@
 
 
 def unpack_call(first, second):
-    shapes = [(240, 960), (240, 320), (240, 320), (240, 960), (16, 256)]
+    shapes = [(240, 960), (320, 240), (320, 240), (240, 960), (16, 256)]
     shapes += [slab_shape(kind) for kind in MLP]
     return pl.pallas_call(
         unpack_kernel,
         out_shape=tuple(jax.ShapeDtypeStruct(s, F32) for s in shapes),
         in_specs=[INV, INV],
         out_specs=[INV] * len(shapes),
+        scratch_shapes=[pltpu.VMEM((256, 768), F32)],
         compiler_params=pltpu.CompilerParams(vmem_limit_bytes=VMEM_LIMIT),
         name="unpack",
     )(first, second)
@@ -1404,7 +1409,7 @@
 
     qt, kv_own, h_one, inverse_one = project_call(x_turned, w_qkv, gains, cosine, sine)
     kv_all, bias, u_all, top, total, wo_all, wg_all, wu_all, wd_turned = forward_call(
-        kv_own, qt, jnp.broadcast_to(owned_positions[None], (8, 128)),
+        kv_own, qt, positions,
         w_output, w_gate, w_up, w_down.T,
     )
     out, h_two, dg, dp, z, dx, a, w_back, delta, gain_two = middle_call(
@@ -1425,7 +1430,7 @@
         sum_query, sum_key, sum_value, sum_output, sum_gains, sum_gate, sum_up, sum_down
     ) = unpack_call(*packed)
     return (
-        out.T[None], grad_in.T[None], sum_query, sum_key, sum_value, sum_output,
+        out.T[None], grad_in.T[None], sum_query, sum_key.T, sum_value.T, sum_output,
         sum_gains[0, :240], sum_gate, sum_up, sum_down.T, sum_gains[1, :240],
     )
 

time: 303 us -> 298 us (0.983)
  local copies, waits for them, and re-layouts: 12.7 us -> 7.75 us
    unnamed x7 -> x5, local copies, waits for them, and re-layouts: 5.88 us -> 2.15 us
where the time goes in v3:
time: 298 us; the launch traced here: 295 us
  Pallas kernels  282 us (95%)
  local copies, waits for them, and re-layouts  7.75 us (3%)
  other arithmetic  3.6 us (1%)
    pallas_call x1, Pallas kernels, backward_call(): pl.pallas_call(backward_kernel, out_shape=(shape((5, 128, ROWS3), F32), s...  92 us
    pallas_call x1, Pallas kernels, last_call(): pl.pallas_call(last_kernel, out_shape=(shape((2, 4, 4, 5, 1, 32, 128), BF...  70.6 us
    pallas_call x1, Pallas kernels, forward_call(): pl.pallas_call(forward_kernel, out_shape=(shape((2, 4, 4, 5, 128, 128), B...  69 us
    pallas_call x1, Pallas kernels, first_call(): pl.pallas_call(first_kernel, out_shape=(jax.ShapeDtypeStruct((960, 1600),...  17.8 us
    pallas_call x1, Pallas kernels, middle_call(): pl.pallas_call(middle_kernel, out_shape=(shape((960, 128), BF16), shape((...  16.3 us
    pallas_call x1, Pallas kernels, unpack_call(): pl.pallas_call(unpack_kernel, out_shape=tuple((jax.ShapeDtypeStruct(s, F3...  7.25 us

profile of v3, /device:TPU:0, one launch (start us, length us, event | category | flops | bytes accessed | tf_op | source)
XLA Modules:
  0.0 294.6 jit_solution(12374319120489013190)
XLA Ops:
  0.6 0.7 convert_bitcast_fusion
  1.3 0.8 multiply_sine_fusion
  2.1 0.7 broadcast_in_dim.8
  2.8 0.8 broadcast_in_dim.9
  3.6 0.7 pad_maximum_fusion.gain_ref
  4.3 1.1 copy.27
  5.4 1.1 copy.28
  6.4 2.0 concatenate.15.w_ref
  8.4 17.8 %gather_first.1 = (bf16[960,1600]{1,0:T(8,128)(2,1)}, bf16[960,128]{1,0:T(8,128)(2,1)}) custom-call(bf16[240,1600]{1,0:T(8,128)(2,1)} %concatenate.15.w_ref, bf16[240,128]{1,0:T(8,128)(2,1)} %pad_maximum_fusion.gain_ref), custom_call_target="tpu_custom_call" | custom-call | tf_op jit(solution)/shard_map/gather_first/pallas_call | solution.py:542
  26.2 3.9 %project.1 = (bf16[5,128,384]{2,1,0:T(8,128)(2,1)}, bf16[5,128,128]{2,1,0:T(8,128)(2,1)}, bf16[960,128]{1,0:T(8,128)(2,1)}, f32[1,128]{1,0:T(1,128)}) custom-call(bf16[960,128]{1,0:T(8,128)(2,1)} %bitcast.23, bf16[960,1600]{1,0:T(8,128)(2,1)} %get-tuple-element.54.w_ref, bf16[960,128]{1,0:T(8,128)(2,1)} %get-tuple-element.53.gain_ref, ...), custom_call_target="tpu_custom_call" | custom-call | tf_op jit(solution)/shard_map/project/pallas_call | solution.py:1226
  30.1 69.0 %attention_forward.1 = (bf16[2,4,4,5,128,128]{5,4,3,2,1,0:T(8,128)(2,1)}, f32[4096,128]{1,0:T(8,128)}, f32[5,128,384]{2,1,0:T(8,128)}, f32[5,1,384]{2,1,0:T(1,12...) custom-call(bf16[5,128,128]{2,1,0:T(8,128)(2,1)} %get-tuple-element., ...), custom_call_target="tpu_custom_call" | custom-call | tf_op jit(solution)/shard_map/attention_forward/pallas_call | solution.py:671
  99.0 16.3 %middle.1 = (bf16[960,128]{1,0:T(8,128)(2,1)}, bf16[960,128]{1,0:T(8,128)(2,1)}, bf16[128,2560]{1,0:T(8,128)(2,1)}, bf16[128,2560]{1,0:T(8,128)(2,1)}, bf16[128,...) custom-call(bf16[960,128]{1,0:T(8,128)(2,1)} %bitcast.24, ...), custom_call_target="tpu_custom_call" | custom-call | tf_op jit(solution)/shard_map/middle/pallas_call | solution.py:1318
  115.4 92.0 %attention_backward.1 = (f32[5,128,384]{2,1,0:T(8,128)}, bf16[5,128,128]{2,1,0:T(8,128)(2,1)}, bf16[5,3,32,128]{3,2,1,0:T(8,128)(2,1)}) custom-call(bf16[2,4,4,5,128,128]{5,4,3,2,1,0:T(8,128)(2,1)} %get-tuple-element.64.kv_ref, bf16[5,128,768]{2,1,0:T(8,128)(2,1)} %get-tuple-element.65.w_ref, f32[4096,128]{1,0:T(8,128)} %get-tuple-element.66.bias_ref, ...), custom_call_target="tpu_custom_call" | custom-call | tf_op jit(solution)/shard_map/attention_backward/pallas_call | solution.py:1027
  207.4 0.0 copy-start
  207.4 5.6 %finish.1 = (bf16[960,128]{1,0:T(8,128)(2,1)}, bf16[960,256]{1,0:T(8,128)(2,1)}, bf16[2560,256]{1,0:T(8,128)(2,1)}, f32[960,1]{1,0:T(8,128)}) custom-call(f32[5,128,384]{2,1,0:T(8,128)} %get-tuple-element.73.dq_ref, bf16[5,128,128]{2,1,0:T(8,128)(2,1)} %get-tuple-element.74.pair_ref, f32[32,128]{1,0:T(8,128)} %get-tuple-element.98.cos_ref, ...), custom_call_target="tpu_custom_call" | custom-call | tf_op jit(solution)/shard_map/finish/pallas_call | solution.py:1374
  213.0 1.2 convert_reduce_fusion.1
  214.2 0.1 concatenate.17
  214.3 0.0 copy-done
  214.3 0.2 convert_reduce_fusion
  214.5 0.1 concatenate.18
  214.7 0.6 pad.4.clone
  215.3 70.6 %last_gradients.1 = (bf16[2,4,4,5,1,32,128]{6,5,4,3,2,1,0:T(8,128)(2,1)}, bf16[2,4,4,5,3,32,128]{6,5,4,3,2,1,0:T(8,128)(2,1)}) custom-call(bf16[960,256]{1,0:T(8,128)(2,1)} %get-tuple-element.80.lhs_ref, bf16[2560,256]{1,0:T(8,128)(2,1)} %get-tuple-element.81.rhs_ref, bf16[64,256]{1,0:T(8,128)(2,1)} %bitcast.29, ...), custom_call_target="tpu_custom_call" | custom-call | tf_op jit(solution)/shard_map/last_gradients/pallas_call | solution.py:1104
  285.9 7.2 %unpack.1 = (f32[240,960]{1,0:T(8,128)}, f32[320,240]{1,0:T(8,128)}, f32[320,240]{1,0:T(8,128)}, f32[240,960]{1,0:T(8,128)}, f32[16,256]{1,0:T(8,128)}, /*index=...) custom-call(bf16[2,4,4,5,1,32,128]{6,5,4,3,2,1,0:T(8,128)(2,1)} %get-tuple-element.85.first, ...), custom_call_target="tpu_custom_call" | custom-call | tf_op jit(solution)/shard_map/unpack/pallas_call | solution.py:1156
  293.1 1.3 fusion
  (3 shorter events, 0.0 us)
Async XLA Ops:
  207.4 6.9 %copy-start = (f32[960,1]{1,0:T(8,128)S(1)}, f32[960,1]{1,0:T(8,128)}, u32[]{:S(2)}) copy-start(f32[960,1]{1,0:T(8,128)} %get-tuple-element.83) | copy-start | bytes 11524
